TPU v7x, 32 devices: a whole 2x2x4 slice. The times are simulated.
32 devices in a mesh: dp: 2 (over y), expert: 16 (over z, x, core).
Axes of the slice: x: 2, y: 2, z: 4, core: 2. Of those that a mesh axis runs over, the one named last changes fastest.
Arguments:
- tokens: bfloat16 [1024, 2048], P('expert'), may hold values from -6 to 6
- attn_gain: float32 [2048], replicated, may hold values from 0.5 to 1.5
- w_query: bfloat16 [2048, 2048], P('expert', 'dp'), may hold values from -0.125 to 0.125
- w_key: bfloat16 [2048, 2048], P('expert', 'dp'), may hold values from -0.125 to 0.125
- w_value: bfloat16 [2048, 2048], P('expert', 'dp'), may hold values from -0.125 to 0.125
- w_out: bfloat16 [2048, 2048], P('expert', 'dp'), may hold values from -0.125 to 0.125
- cache: bfloat16 [32768, 4096], P('expert', 'dp')
- page_table: int32 [16, 16], P('expert'), may hold values from 0 to 15, each once within a row
- cache_len: int32 [16, 4], P('expert'), may hold values from 1 to 512, 1024 in all within a row
- new_len: int32 [16, 4], P('expert'), may hold values from 1 to 32, 64 in all within a row
- kv_owner: int32 [1024, 1], P('expert'), may hold values from 0 to 15; in each aligned block of 64 rows (0 to 63, 64 to 127, ...) at most 8 rows name the same one
- moe_gain: float32 [2048], replicated, may hold values from 0.5 to 1.5
- w_gate: bfloat16 [16, 2048, 1024], P('expert', None, 'dp'), may hold values from -0.125 to 0.125
- w_up: bfloat16 [16, 2048, 1024], P('expert', None, 'dp'), may hold values from -0.125 to 0.125
- w_down: bfloat16 [16, 1024, 2048], P('expert', 'dp'), may hold values from -0.1875 to 0.1875
- expert_ids: int32 [1024, 8], P('expert'), may hold values from 0 to 15, all different within a row; in each aligned block of 64 rows (0 to 63, 64 to 127, ...) at most 64 rows name the same one
- gate_weights: float32 [1024, 8], P('expert'), may hold values from 0.05 to 0.5
Outputs:
- out: bfloat16 [1024, 2048], P('expert')
- new_rows: bfloat16 [2048, 4096], P('expert', 'dp')
Inputs may be any that keep to these rules, and one draw needn't show every extreme that they name: `page_table`: each row of one index of the expert axis lists every local page once; request r reserves the pages in entries r * 4 to (r+1) * 4 - 1. `cache_len`: the lengths of one index sum to 4 * 4 * 128 // 2, and one of them equals 512. `new_len`: the new tokens of one index sum to 64 and stand request by request; one request has exactly 64 // 2. `kv_owner`: among the rows of one device no owner is named more than 8 times; some owner is named exactly 8 times. `expert_ids`: each row names distinct experts; among the rows of one device no expert is named more than 64 times, a bound that some block reaches.
All inputs are finite; a program needn't handle non-finite values.
Results may differ from a plain program's by a relative error of at most 0.012.
The roundings to bfloat16 on the way count: a program that leaves them out, or rounds other values in their place, can miss the bound.
Values may be sent and summed in bfloat16 or wider, within the bound.
A program may use at most 128 MiB of HBM per device.

v0:
```python
import jax
import jax.numpy as jnp
from jax import lax
from jax.sharding import PartitionSpec as P

HD = 128
PAGE = 128


EPSILON = 1e-05


def norm_rows(row_data, gain_vec):
    mean_sq = jnp.mean(row_data * row_data, axis=-1, keepdims=True)
    return (row_data * lax.rsqrt(mean_sq + EPSILON) * gain_vec).astype(jnp.bfloat16)


def route_rank(route_ids, block_rows, id_range):
    row_total = route_ids.shape[0]
    labels = jnp.arange(id_range, dtype=jnp.int32)
    counts = jnp.sum((route_ids[:, :, None] == labels[None, None, :]).astype(jnp.int32), axis=1)
    counts = counts.reshape(row_total // block_rows, block_rows, id_range)
    before = (jnp.cumsum(counts, axis=1) - counts).reshape(row_total, id_range)
    return jnp.take_along_axis(before, route_ids, axis=1)


def key_masks(table_row, cache_lens, new_lens, row_count, page_size):
    req_count = cache_lens.shape[0]
    pages_here = table_row.shape[0]
    per_request = pages_here // req_count
    slot_ids = jnp.arange(pages_here, dtype=jnp.int32)
    matches = (table_row[:, None] == slot_ids[None, :]).astype(jnp.int32)
    slot_of_page = jnp.sum(matches * slot_ids[:, None], axis=0)
    page_request = slot_of_page // per_request
    page_start = slot_of_page % per_request * page_size
    key_request = jnp.repeat(page_request, page_size)
    key_position = jnp.repeat(page_start, page_size) + jnp.tile(
        jnp.arange(page_size, dtype=jnp.int32), pages_here
    )
    request_ids = jnp.arange(req_count, dtype=jnp.int32)
    key_length = jnp.sum(
        (key_request[:, None] == request_ids[None, :]).astype(jnp.int32) * cache_lens[None, :],
        axis=1,
    )
    request_ends = jnp.cumsum(new_lens)
    tok_ids = jnp.arange(row_count, dtype=jnp.int32)
    tok_request = jnp.sum((tok_ids[:, None] >= request_ends[None, :]).astype(jnp.int32), axis=1)
    cached = (tok_request[:, None] == key_request[None, :]) & (key_position < key_length)[None, :]
    fresh_mask = tok_request[:, None] == tok_request[None, :]
    return jnp.concatenate([cached, fresh_mask], axis=1)


def expert_block(routed, w_gate, w_up, w_down):
    gate_proj = jnp.einsum("necd,edf->necf", routed, w_gate, preferred_element_type=jnp.float32)
    up_proj = jnp.einsum("necd,edf->necf", routed, w_up, preferred_element_type=jnp.float32)
    active = (jax.nn.silu(gate_proj) * up_proj).astype(jnp.bfloat16)
    return jnp.einsum("necf,efd->necd", active, w_down, preferred_element_type=jnp.float32).astype(
        jnp.bfloat16
    )


def local(
    tokens,
    attn_gain,
    w_query,
    w_key,
    w_value,
    w_out,
    cache,
    page_table,
    cache_len,
    new_len,
    kv_owner,
    moe_gain,
    w_gate,
    w_up,
    w_down,
    expert_ids,
    gate_weights,
):
    row_count, model_width = tokens.shape
    n_expert = lax.axis_size("expert")
    local_experts = w_gate.shape[0]
    experts_all = n_expert * local_experts
    top_count = expert_ids.shape[1]
    capacity = min(row_count, 2 * row_count * top_count // experts_all)
    kv_cap = max(2, 2 * row_count // n_expert)
    head_group = w_query.shape[1] // HD
    full_query, full_key, full_value, full_out = (
        lax.all_gather(w_query, "expert", axis=0, tiled=True),
        lax.all_gather(w_key, "expert", axis=0, tiled=True),
        lax.all_gather(w_value, "expert", axis=0, tiled=True),
        lax.all_gather(w_out, "expert", axis=0, tiled=True),
    )
    resid_in = tokens.astype(jnp.float32)
    normed = norm_rows(resid_in, attn_gain)
    queries = jnp.dot(normed, full_query, preferred_element_type=jnp.float32).astype(jnp.bfloat16)
    new_keys = jnp.dot(normed, full_key, preferred_element_type=jnp.float32).astype(jnp.bfloat16)
    new_values = jnp.dot(normed, full_value, preferred_element_type=jnp.float32).astype(
        jnp.bfloat16
    )
    cache_count = cache.shape[0]
    split_cache = cache.reshape(cache_count, 2, head_group, HD)
    all_keys = jnp.concatenate(
        [split_cache[:, 0], new_keys.reshape(row_count, head_group, HD)], axis=0
    )
    all_values = jnp.concatenate(
        [split_cache[:, 1], new_values.reshape(row_count, head_group, HD)], axis=0
    )
    scores = jnp.einsum(
        "thc,rhc->htr",
        queries.reshape(row_count, head_group, HD),
        all_keys,
        preferred_element_type=jnp.float32,
    ) * HD ** (-0.5)
    valid_mask = key_masks(page_table[0], cache_len[0], new_len[0], row_count, PAGE)
    scores = jnp.where(valid_mask[None, :, :], scores, -1e30)
    highest = jnp.max(scores, axis=-1, keepdims=True)
    weights = jnp.exp(scores - highest)
    probs = (weights / jnp.sum(weights, axis=-1, keepdims=True)).astype(jnp.bfloat16)
    heads_out = (
        jnp.einsum("htr,rhc->thc", probs, all_values, preferred_element_type=jnp.float32)
        .astype(jnp.bfloat16)
        .reshape(row_count, head_group * HD)
    )
    attn_part = jnp.einsum("tc,dc->td", heads_out, full_out, preferred_element_type=jnp.float32)
    attn_out = lax.psum(attn_part.astype(jnp.bfloat16), "dp").astype(jnp.float32)
    residual = resid_in + attn_out
    moe_in = norm_rows(residual, moe_gain)
    kv_row = jnp.concatenate([new_keys, new_values], axis=1)
    kv_rank = route_rank(kv_owner, row_count, n_expert)[:, 0]
    kv_buffer = (
        jnp.zeros((n_expert, kv_cap, kv_row.shape[1]), jnp.bfloat16)
        .at[kv_owner[:, 0], kv_rank]
        .set(kv_row)
    )
    slot_rank = route_rank(expert_ids, row_count, experts_all)
    spread_rows = jnp.broadcast_to(moe_in[:, None, :], (row_count, top_count, model_width))
    tok_buffer = (
        jnp.zeros((experts_all, capacity, model_width), jnp.bfloat16)
        .at[expert_ids, slot_rank]
        .set(spread_rows)
    )
    tok_buffer = tok_buffer.reshape(n_expert, local_experts, capacity, model_width)
    got_rows, got_kv = (
        lax.all_to_all(tok_buffer, "expert", split_axis=0, concat_axis=0, tiled=True),
        lax.all_to_all(kv_buffer, "expert", split_axis=0, concat_axis=0, tiled=True),
    )
    partial_value = expert_block(got_rows, w_gate, w_up, w_down)
    returned = lax.all_to_all(
        partial_value, "expert", split_axis=0, concat_axis=0, tiled=True
    ).reshape(experts_all, capacity, model_width)
    picked = returned[expert_ids, slot_rank].astype(jnp.float32)
    moe_part = jnp.sum(picked * gate_weights[:, :, None], axis=1)
    moe_total = lax.psum(moe_part.astype(jnp.bfloat16), "dp").astype(jnp.float32)
    out = (residual + moe_total).astype(jnp.bfloat16)
    new_rows = got_kv.reshape(n_expert * kv_cap, kv_row.shape[1])
    return (out, new_rows)


def solution(mesh):
    placed = (
        P("expert", None),
        P(),
        P("expert", "dp"),
        P("expert", "dp"),
        P("expert", "dp"),
        P("expert", "dp"),
        P("expert", "dp"),
        P("expert", None),
        P("expert", None),
        P("expert", None),
        P("expert", None),
        P(),
        P("expert", None, "dp"),
        P("expert", None, "dp"),
        P("expert", "dp", None),
        P("expert", None),
        P("expert", None),
    )
    return jax.shard_map(
        local,
        mesh=mesh,
        in_specs=placed,
        out_specs=(P("expert", None), P("expert", "dp")),
        check_vma=False,
    )
```

profile of v0, /device:TPU:0, one launch (start us, length us, event | category | flops | bytes accessed | tf_op | source)
XLA Modules:
  0.0 608.7 jit_solution(15766272843035560138)
XLA Ops:
  10.0 12.3 %copy.69 = bf16[2048,2048]{0,1:T(8,128)(2,1)} copy(bf16[2048,2048]{1,0:T(8,128)(2,1)} %param.23) | data formatting | bytes 16777216 | tf_op args[6]
  22.4 6.2 %fusion.77 = (bf16[2048,1,8,128]{0,3,2,1:T(8,128)(2,1)}, bf16[2048,1,8,128]{0,3,2,1:T(8,128)(2,1)}) fusion(bf16[2048,2,8,128]{0,3,2,1:T(8,128)(2,1)} %bitcast.163), kind=kLoop, calls=%fused_computation.115 | loop fusion | bytes 16777216 | tf_op jit(solution)/shard_map/slice | solution.py:105
  28.5 6.5 %copy.84 = bf16[2048,1,8,128]{3,0,2,1:T(8,128)(2,1)} copy(bf16[2048,1,8,128]{0,3,2,1:T(8,128)(2,1)} %get-tuple-element.2) | data formatting | bytes 8388608
  35.0 6.7 %copy.85 = bf16[2048,1,8,128]{3,0,2,1:T(8,128)(2,1)} copy(bf16[2048,1,8,128]{0,3,2,1:T(8,128)(2,1)} %get-tuple-element.3) | data formatting | bytes 8388608
  42.8 20.7 %all-gather.9.cloned.1.call-done = bf16[2048,1024]{1,0:T(8,128)(2,1)} async-done(((bf16[128,1024]{1,0:T(8,128)(2,1)}), bf16[2048,1024]{1,0:T(8,128)(2,1)}) %all-gather.9.cloned.1.call-update) | async-done | bytes 4194320 | tf_op jit(solution)/shard_map/all_gather | solution.py:91
  63.5 3.1 convolution_convert_fusion.1
  66.6 48.1 %all-gather.5.cloned.1.call-done = bf16[2048,1024]{1,0:T(8,128)(2,1)} async-done(((bf16[128,1024]{1,0:T(8,128)(2,1)}), bf16[2048,1024]{1,0:T(8,128)(2,1)}) %all-gather.5.cloned.1.call-update) | async-done | bytes 4194320 | tf_op jit(solution)/shard_map/all_gather | solution.py:92
  114.7 3.1 convolution_convert_fusion.3
  117.8 48.1 %all-gather.7.cloned.1.call-done = bf16[2048,1024]{1,0:T(8,128)(2,1)} async-done(((bf16[128,1024]{1,0:T(8,128)(2,1)}), bf16[2048,1024]{1,0:T(8,128)(2,1)}) %all-gather.7.cloned.1.call-update) | async-done | bytes 4194320 | tf_op jit(solution)/shard_map/all_gather | solution.py:90
  166.0 3.2 fusion.35
  169.4 3.0 fusion.2
  172.5 4.4 fusion.78
  176.9 6.1 %fusion.36 = bf16[8,8,8,128]{3,2,1,0:T(8,128)(2,1)S(1)} fusion(bf16[64,8,128]{2,0,1:T(8,128)(2,1)S(1)} %copy_bitcast_fusion, bf16[2048,8,128]{2,0,1:T(8,128)(2,1)} %bitcast.164, f32[8,64]{1,0:T(8,128)S(1)} %fusion.78, f32[8,64,2112]{2,1,0:T(8,128)} %fusion.2), kind=kOutput, calls=%fused_computation.42 | convolution fusion | flops 288787008 | bytes 8783872 | tf_op jit(solution)/shard_map/htr,rhc->thc/dot_general | solution.py:122
  183.0 34.1 %all-gather.11.cloned.1.call-done = bf16[2048,1024]{1,0:T(8,128)(2,1)} async-done(((bf16[128,1024]{1,0:T(8,128)(2,1)}), bf16[2048,1024]{1,0:T(8,128)(2,1)}) %all-gather.11.cloned.1.call-update) | async-done | bytes 4194320 | tf_op jit(solution)/shard_map/all_gather | solution.py:93
  217.1 4.3 convolution_convert_fusion
  221.8 3.8 gather_fusion.1
  225.9 17.3 %all-reduce.3.cloned.1.call-done = bf16[64,2048]{1,0:T(8,128)(2,1)} async-done(((bf16[64,2048]{1,0:T(8,128)(2,1)}), bf16[64,2048]{1,0:T(8,128)(2,1)}) %all-reduce.3.cloned.1.call-update) | async-done | bytes 262160 | tf_op jit(solution)/shard_map/psum | solution.py:127
  245.5 1.6 broadcast_bitcast_fusion
  247.1 2.4 broadcast_in_dim.35
  249.6 92.0 %scatter_fusion = bf16[16,64,2048]{2,1,0:T(8,128)(2,1)} fusion(bf16[16,64,2048]{2,1,0:T(8,128)(2,1)} %broadcast_in_dim.35, s32[512]{0:T(512)S(1)} %reshape.227, bf16[512,2048]{1,0:T(8,128)(2,1)} %broadcast_bitcast_fusion), kind=kCustom, calls=%fused_computation.3 | custom fusion | bytes 6295552 | tf_op jit(solution)/shard_map/scatter | solution.py:142
  341.6 98.0 %all_to_all.15 = bf16[16,1,64,2048]{3,2,1,0:T(8,128)(2,1)S(1)} all-to-all(bf16[16,1,64,2048]{3,2,1,0:T(8,128)(2,1)} %bitcast.162), channel_id=1, replica_groups=mesh['dp'=2,'expert'=16] {'expert'}, dimensions={0} | all-to-all | bytes 8388608 | tf_op jit(solution)/shard_map/all_to_all | solution.py:146
  439.6 2.0 copy-done.3
  441.6 3.7 fusion.14
  445.3 10.0 %convert_bitcast_fusion = bf16[16,1,64,2048]{3,2,1,0:T(8,128)(2,1)} fusion(bf16[1,512,2048]{2,1,0:T(8,128)(2,1)S(1)} %copy-done, bf16[1,2048,512]{2,1,0:T(8,128)(2,1)} %param.30, bf16[16,1,64,2048]{3,2,1,0:T(8,128)(2,1)} %copy-done.3, f32[16,64,512]{2,1,0:T(8,128)} %fusion.14), kind=kOutput, calls=%fused_computation.24 | convolution fusion | flops 4300210176 | bytes 14680064 | tf_op jit(solution)/shard_map/necf,efd->necd/dot_general | solution.py:57
  455.2 5.5 all-to-all-start.1
  462.8 11.6 %scatter_fusion.1 = bf16[16,8,2048]{2,1,0:T(8,128)(2,1)} fusion(bf16[16,8,2048]{2,1,0:T(8,128)(2,1)} %broadcast_in_dim.40, s32[64]{0:T(128)S(1)} %fusion.65, bf16[64,2048]{1,0:T(8,128)(2,1)S(1)} %pad_maximum_fusion), kind=kCustom, calls=%fused_computation.4 | custom fusion | bytes 786944 | tf_op jit(solution)/shard_map/scatter | solution.py:135
  474.4 64.0 %all-to-all-done.1 = bf16[16,1,64,2048]{3,2,1,0:T(8,128)(2,1)} async-done(((bf16[16,1,64,2048]{3,2,1,0:T(8,128)(2,1)}), bf16[16,1,64,2048]{3,2,1,0:T(8,128)(2,1)}, u32[]{:S(2)}, u32[]{:S(2)}) %all-to-all-start.1) | async-done | bytes 4194336 | tf_op jit(solution)/shard_map/all_to_all | solution.py:150
  538.4 19.6 %all-to-all-start.2 = ((bf16[16,8,2048]{2,1,0:T(8,128)(2,1)}), bf16[16,8,2048]{2,1,0:T(8,128)(2,1)S(1)}, u32[]{:S(2)}, u32[]{:S(2)}) async-start(bf16[16,8,2048]{2,1,0:T(8,128)(2,1)} %scatter_fusion.1), calls=%async_computation.2 | async-start | bytes 1048576 | tf_op jit(solution)/shard_map/all_to_all | solution.py:147
  558.4 13.0 %gather_fusion = bf16[512,2048]{1,0:T(8,128)(2,1)} fusion(bf16[16,64,2048]{2,1,0:T(8,128)(2,1)} %bitcast.34, s32[512]{0:T(512)S(1)} %reshape.207), kind=kCustom, calls=%fused_computation | custom fusion | bytes 4198400 | tf_op jit(solution)/shard_map/gather | solution.py:153
  571.4 4.1 fusion.11
  575.6 23.7 %all-reduce.5.cloned.1.call-done = bf16[64,2048]{1,0:T(8,128)(2,1)} async-done(((bf16[64,2048]{1,0:T(8,128)(2,1)}), bf16[64,2048]{1,0:T(8,128)(2,1)}) %all-reduce.5.cloned.1.call-update) | async-done | bytes 262160 | tf_op jit(solution)/shard_map/psum | solution.py:155
  599.3 1.8 add_convert_fusion
  (84 shorter events, 10.1 us)
Async XLA Ops:
  7.2 438.1 %copy-start = (bf16[1,512,2048]{2,1,0:T(8,128)(2,1)S(1)}, bf16[1,512,2048]{2,1,0:T(8,128)(2,1)}, u32[]{:S(2)}) copy-start(bf16[1,512,2048]{2,1,0:T(8,128)(2,1)} %param.31) | copy-start | bytes 6291460
  7.2 56.3 %all-gather.9.cloned.1.call-start = ((), (), s32[]{:S(2)}) async-start(), calls=%async_computation.5 | async-start | bytes 4456448 | tf_op jit(solution)/shard_map/all_gather | solution.py:91
  7.9 106.8 %all-gather.5.cloned.1.call-start = ((), (), s32[]{:S(2)}) async-start(), calls=%async_computation.3 | async-start | bytes 4456448 | tf_op jit(solution)/shard_map/all_gather | solution.py:92
  8.7 157.3 %all-gather.7.cloned.1.call-start = ((), (), s32[]{:S(2)}) async-start(), calls=%async_computation.4 | async-start | bytes 4456448 | tf_op jit(solution)/shard_map/all_gather | solution.py:90
  9.4 207.7 %all-gather.11.cloned.1.call-start = ((), (), s32[]{:S(2)}) async-start(), calls=%async_computation.6 | async-start | bytes 4456448 | tf_op jit(solution)/shard_map/all_gather | solution.py:93
  10.0 233.3 %all-reduce.3.cloned.1.call-start = ((), (), s32[]{:S(2)}) async-start(), calls=%async_computation.7 | async-start | bytes 524288 | tf_op jit(solution)/shard_map/psum | solution.py:127
  35.0 6.7 %copy-start.12 = (s32[1,4]{1,0:T(1,128)S(1)}, s32[1,4]{1,0:T(1,128)}, u32[]{:S(2)}) copy-start(s32[1,4]{1,0:T(1,128)} %param.26) | copy-start | bytes 52
  35.0 6.9 %copy-start.13 = (s32[1,16]{1,0:T(1,128)S(1)}, s32[1,16]{1,0:T(1,128)}, u32[]{:S(2)}) copy-start(s32[1,16]{1,0:T(1,128)} %param.24) | copy-start | bytes 196
  35.0 7.2 %copy-start.10 = (s32[1,4]{1,0:T(1,128)S(1)}, s32[1,4]{1,0:T(1,128)}, u32[]{:S(2)}) copy-start(s32[1,4]{1,0:T(1,128)} %param.25) | copy-start | bytes 52
  35.0 7.3 %copy-start.1 = (bf16[64,2048]{1,0:T(8,128)(2,1)S(1)}, bf16[64,2048]{1,0:T(8,128)(2,1)}, u32[]{:S(2)}) copy-start(bf16[64,2048]{1,0:T(8,128)(2,1)} %param.17) | copy-start | bytes 786436
  35.0 7.4 %copy-start.6 = (s32[64,8]{0,1:T(8,128)S(1)}, s32[64,8]{0,1:T(8,128)}, u32[]{:S(2)}) copy-start(s32[64,8]{0,1:T(8,128)} %param.32) | copy-start | bytes 6148
  35.0 28.4 %copy-start.5 = (f32[2048]{0:T(1024)S(1)}, f32[2048]{0:T(1024)}, u32[]{:S(2)}) copy-start(f32[2048]{0:T(1024)} %param.18) | copy-start | bytes 24580
  166.0 3.4 copy-start.2
  221.8 22.6 %copy-start.7 = (f32[2048]{0:T(1024)S(1)}, f32[2048]{0:T(1024)}, u32[]{:S(2)}) copy-start(f32[2048]{0:T(1024)} %param.28) | copy-start | bytes 24580
  341.6 100.0 %copy-start.11 = (bf16[1,2048,512]{2,1,0:T(8,128)(2,1)S(1)}, bf16[1,2048,512]{2,1,0:T(8,128)(2,1)}, u32[]{:S(2)}) copy-start(bf16[1,2048,512]{2,1,0:T(8,128)(2,1)} %param.29) | copy-start | bytes 6291460
  439.6 2.0 copy-start.3
  455.2 5.5 copy-start.9
  455.2 83.2 %all-to-all-start.1 = ((bf16[16,1,64,2048]{3,2,1,0:T(8,128)(2,1)}), bf16[16,1,64,2048]{3,2,1,0:T(8,128)(2,1)}, u32[]{:S(2)}, u32[]{:S(2)}) async-start(bf16[16,1,64,2048]{3,2,1,0:T(8,128)(2,1)} %convert_bitcast_fusion), calls=%async_computation.1 | async-start | bytes 8388608 | tf_op jit(solution)/shard_map/all_to_all | solution.py:150
  460.8 97.6 %copy-start.8 = (f32[64,8]{0,1:T(8,128)S(1)}, f32[64,8]{0,1:T(8,128)}, u32[]{:S(2)}) copy-start(f32[64,8]{0,1:T(8,128)} %param.33) | copy-start | bytes 6148
  538.4 37.2 %all-to-all-start.2 = ((bf16[16,8,2048]{2,1,0:T(8,128)(2,1)}), bf16[16,8,2048]{2,1,0:T(8,128)(2,1)S(1)}, u32[]{:S(2)}, u32[]{:S(2)}) async-start(bf16[16,8,2048]{2,1,0:T(8,128)(2,1)} %scatter_fusion.1), calls=%async_computation.2 | async-start | bytes 1048576 | tf_op jit(solution)/shard_map/all_to_all | solution.py:147
  558.1 41.2 %all-reduce.5.cloned.1.call-start = ((), (), s32[]{:S(2)}) async-start(), calls=%async_computation.8 | async-start | bytes 524288 | tf_op jit(solution)/shard_map/psum | solution.py:155
  558.4 40.9 %copy-start.4 = (bf16[64,2048]{1,0:T(8,128)(2,1)S(1)}, bf16[64,2048]{1,0:T(8,128)(2,1)}, u32[]{:S(2)}) copy-start(bf16[64,2048]{1,0:T(8,128)(2,1)} %all-reduce.3.cloned.1.call-done) | copy-start | bytes 786436
Sparse Core Ops, SparseCore 0:
  10.2 53.2 all-gather.8
  65.6 49.0 all-gather.4
  116.9 49.0 all-gather.6
  168.0 49.0 all-gather.10
  221.5 21.6 all-reduce.2
  575.7 23.5 all-reduce.4
where the time goes:
time: 612 us; the launch traced here: 609 us
  waiting for transfers between devices  259 us (42%)
  local copies, waits for them, and re-layouts  162 us (26%)
  blocking collectives  98 us (16%)
  matrix products  40.9 us (7%)
  starting transfers between devices  25.4 us (4%)
  between operations  14.4 us (2%)
  other arithmetic  9.51 us (2%)
    all_to_all x1, blocking collectives, local(): lax.all_to_all(tok_buffer, 'expert', split_axis=0, concat_axis=0, tiled=T...  98 us
    scatter x1, local copies, waits for them, and re-layouts, local(): tok_buffer = jnp.zeros((experts_all, capacity, model_width), jnp.bfloat16...  92 us
    all_to_all x1, waiting for transfers between devices, local(): lax.all_to_all(partial_value, 'expert', split_axis=0, concat_axis=0, tile...  64 us
    all_gather x1, waiting for transfers between devices, local(): lax.all_gather(w_query, 'expert', axis=0, tiled=True)  48.1 us
    all_gather x1, waiting for transfers between devices, local(): lax.all_gather(w_value, 'expert', axis=0, tiled=True)  48.1 us
    all_gather x1, waiting for transfers between devices, local(): lax.all_gather(w_out, 'expert', axis=0, tiled=True)  34.1 us
    unnamed x34, local copies, waits for them, and re-layouts  28.6 us
    psum x1, waiting for transfers between devices, local(): lax.psum(moe_part.astype(jnp.bfloat16), 'dp').astype(jnp.float32)  23.7 us
  transfers between devices with their start and end apart: 8, of which 7 were waited for; matrix products, arithmetic and copies ran while one was open for 15% of the time, Pallas kernels for 0%

commit v1 on v0

--- a/solution.py
+++ b/solution.py
@@ -15,13 +15,10 @@
     return (row_data * lax.rsqrt(mean_sq + EPSILON) * gain_vec).astype(jnp.bfloat16)
 
 
-def route_rank(route_ids, block_rows, id_range):
-    row_total = route_ids.shape[0]
-    labels = jnp.arange(id_range, dtype=jnp.int32)
-    counts = jnp.sum((route_ids[:, :, None] == labels[None, None, :]).astype(jnp.int32), axis=1)
-    counts = counts.reshape(row_total // block_rows, block_rows, id_range)
-    before = (jnp.cumsum(counts, axis=1) - counts).reshape(row_total, id_range)
-    return jnp.take_along_axis(before, route_ids, axis=1)
+def owner_rank(owners):
+    ids = jnp.arange(owners.shape[0], dtype=jnp.int32)
+    same = (owners[:, None] == owners[None, :]) & (ids[None, :] < ids[:, None])
+    return jnp.sum(same.astype(jnp.int32), axis=1)
 
 
 def key_masks(table_row, cache_lens, new_lens, row_count, page_size):
@@ -42,21 +39,14 @@
         (key_request[:, None] == request_ids[None, :]).astype(jnp.int32) * cache_lens[None, :],
         axis=1,
     )
-    request_ends = jnp.cumsum(new_lens)
+    request_ends = jnp.sum(
+        jnp.where(request_ids[None, :] <= request_ids[:, None], new_lens[None, :], 0), axis=1
+    )
     tok_ids = jnp.arange(row_count, dtype=jnp.int32)
     tok_request = jnp.sum((tok_ids[:, None] >= request_ends[None, :]).astype(jnp.int32), axis=1)
     cached = (tok_request[:, None] == key_request[None, :]) & (key_position < key_length)[None, :]
     fresh_mask = tok_request[:, None] == tok_request[None, :]
     return jnp.concatenate([cached, fresh_mask], axis=1)
-
-
-def expert_block(routed, w_gate, w_up, w_down):
-    gate_proj = jnp.einsum("necd,edf->necf", routed, w_gate, preferred_element_type=jnp.float32)
-    up_proj = jnp.einsum("necd,edf->necf", routed, w_up, preferred_element_type=jnp.float32)
-    active = (jax.nn.silu(gate_proj) * up_proj).astype(jnp.bfloat16)
-    return jnp.einsum("necf,efd->necd", active, w_down, preferred_element_type=jnp.float32).astype(
-        jnp.bfloat16
-    )
 
 
 def local(
@@ -82,8 +72,6 @@
     n_expert = lax.axis_size("expert")
     local_experts = w_gate.shape[0]
     experts_all = n_expert * local_experts
-    top_count = expert_ids.shape[1]
-    capacity = min(row_count, 2 * row_count * top_count // experts_all)
     kv_cap = max(2, 2 * row_count // n_expert)
     head_group = w_query.shape[1] // HD
     full_query, full_key, full_value, full_out = (
@@ -128,33 +116,37 @@
     residual = resid_in + attn_out
     moe_in = norm_rows(residual, moe_gain)
     kv_row = jnp.concatenate([new_keys, new_values], axis=1)
-    kv_rank = route_rank(kv_owner, row_count, n_expert)[:, 0]
-    kv_buffer = (
-        jnp.zeros((n_expert, kv_cap, kv_row.shape[1]), jnp.bfloat16)
-        .at[kv_owner[:, 0], kv_rank]
-        .set(kv_row)
+    kv_slot = kv_owner[:, 0] * kv_cap + owner_rank(kv_owner[:, 0])
+    slots = jnp.arange(n_expert * kv_cap, dtype=jnp.int32)
+    kv_buffer = jnp.dot(
+        (slots[:, None] == kv_slot[None, :]).astype(jnp.bfloat16),
+        kv_row,
+        preferred_element_type=jnp.float32,
+    ).astype(jnp.bfloat16)
+    labels = jnp.arange(experts_all, dtype=jnp.int32)
+    gates = jnp.sum(
+        jnp.where(expert_ids[:, :, None] == labels, gate_weights[:, :, None], 0.0), axis=1
     )
-    slot_rank = route_rank(expert_ids, row_count, experts_all)
-    spread_rows = jnp.broadcast_to(moe_in[:, None, :], (row_count, top_count, model_width))
-    tok_buffer = (
-        jnp.zeros((experts_all, capacity, model_width), jnp.bfloat16)
-        .at[expert_ids, slot_rank]
-        .set(spread_rows)
+    new_rows = lax.all_to_all(
+        kv_buffer.reshape(n_expert, kv_cap, -1), "expert", split_axis=0, concat_axis=0, tiled=True
+    ).reshape(n_expert * kv_cap, -1)
+    all_gates = lax.all_gather(gates, "expert", axis=0, tiled=True)
+    rows = lax.all_gather(moe_in, "expert", axis=0, tiled=True)
+    first = lax.axis_index("expert") * local_experts
+    gated = 0.0
+    for local_id in range(local_experts):
+        gate_proj = jnp.dot(rows, w_gate[local_id], preferred_element_type=jnp.float32)
+        up_proj = jnp.dot(rows, w_up[local_id], preferred_element_type=jnp.float32)
+        active = (jax.nn.silu(gate_proj) * up_proj).astype(jnp.bfloat16)
+        part = jnp.dot(active, w_down[local_id], preferred_element_type=jnp.float32)
+        part = part.astype(jnp.bfloat16).astype(jnp.float32)
+        mine = jnp.sum(jnp.where(labels == first + local_id, all_gates, 0.0), axis=1)
+        gated = gated + part * mine[:, None]
+    moe_part = lax.psum_scatter(
+        gated.astype(jnp.bfloat16), "expert", scatter_dimension=0, tiled=True
     )
-    tok_buffer = tok_buffer.reshape(n_expert, local_experts, capacity, model_width)
-    got_rows, got_kv = (
-        lax.all_to_all(tok_buffer, "expert", split_axis=0, concat_axis=0, tiled=True),
-        lax.all_to_all(kv_buffer, "expert", split_axis=0, concat_axis=0, tiled=True),
-    )
-    partial_value = expert_block(got_rows, w_gate, w_up, w_down)
-    returned = lax.all_to_all(
-        partial_value, "expert", split_axis=0, concat_axis=0, tiled=True
-    ).reshape(experts_all, capacity, model_width)
-    picked = returned[expert_ids, slot_rank].astype(jnp.float32)
-    moe_part = jnp.sum(picked * gate_weights[:, :, None], axis=1)
-    moe_total = lax.psum(moe_part.astype(jnp.bfloat16), "dp").astype(jnp.float32)
+    moe_total = lax.psum(moe_part, "dp").astype(jnp.float32)
     out = (residual + moe_total).astype(jnp.bfloat16)
-    new_rows = got_kv.reshape(n_expert * kv_cap, kv_row.shape[1])
     return (out, new_rows)
 
 

time: 612 us -> 420 us (0.69)
  local copies, waits for them, and re-layouts: 162 us -> 33.6 us
  blocking collectives: 98 us -> 22.1 us
  waiting for transfers between devices: 259 us -> 294 us
  starting transfers between devices: 25.4 us -> 3.89 us
    scatter x2 -> x0, local copies, waits for them, and re-layouts: 104 us -> none  [the longest x1 92 us: local(): tok_buffer = jnp.zeros((experts_all, capacity, model_width), jnp.bfloat16...]
    all_to_all x1 -> x0, blocking collectives: 98 us -> none  [local(): lax.all_to_all(tok_buffer, 'expert', split_axis=0, concat_axis=0, tiled=T...]
    reduce_scatter x0 -> x1, waiting for transfers between devices: none -> 65.8 us  [local(): lax.psum_scatter(gated.astype(jnp.bfloat16), 'expert', scatter_dimension=...]
    all_to_all x2 -> x1, waiting for transfers between devices: 64 us -> 0.01 us  [local(): lax.all_to_all(kv_buffer.reshape(n_expert, kv_cap, -1), 'expert', split_a...]
    all_gather x0 -> x1, waiting for transfers between devices: none -> 28.4 us  [local(): rows = lax.all_gather(moe_in, 'expert', axis=0, tiled=True)]
    all_gather x0 -> x1, blocking collectives: none -> 22.1 us  [local(): all_gates = lax.all_gather(gates, 'expert', axis=0, tiled=True)]
    all_to_all x2 -> x1, starting transfers between devices: 25.1 us -> 3.58 us  [local(): lax.all_to_all(kv_buffer.reshape(n_expert, kv_cap, -1), 'expert', split_a...]
    gather x7 -> x0, local copies, waits for them, and re-layouts: 17.9 us -> none  [the longest x1 13 us: local(): picked = returned[expert_ids, slot_rank].astype(jnp.float32)]
  transfers between devices with their start and end apart: 8 -> 9, of which waited for: 7 -> 8; matrix products, arithmetic and copies ran while one was open for 15% -> 14% of each run, Pallas kernels for 0% -> 0%
where the time goes in v1:
time: 420 us; the launch traced here: 419 us
  waiting for transfers between devices  294 us (70%)
  matrix products  44.9 us (11%)
  local copies, waits for them, and re-layouts  33.6 us (8%)
  blocking collectives  22.1 us (5%)
  between operations  14.4 us (3%)
  other arithmetic  5.82 us (1%)
    reduce_scatter x1, waiting for transfers between devices, local(): lax.psum_scatter(gated.astype(jnp.bfloat16), 'expert', scatter_dimension=...  65.8 us
    all_gather x1, waiting for transfers between devices, local(): lax.all_gather(w_query, 'expert', axis=0, tiled=True)  48.1 us
    all_gather x1, waiting for transfers between devices, local(): lax.all_gather(w_value, 'expert', axis=0, tiled=True)  48.1 us
    all_gather x1, waiting for transfers between devices, local(): lax.all_gather(w_out, 'expert', axis=0, tiled=True)  34.1 us
    all_gather x1, waiting for transfers between devices, local(): rows = lax.all_gather(moe_in, 'expert', axis=0, tiled=True)  28.4 us
    unnamed x29, local copies, waits for them, and re-layouts  27.3 us
    psum x1, waiting for transfers between devices, local(): moe_total = lax.psum(moe_part, 'dp').astype(jnp.float32)  24.4 us
    all_gather x1, blocking collectives, local(): all_gates = lax.all_gather(gates, 'expert', axis=0, tiled=True)  22.1 us
  transfers between devices with their start and end apart: 9, of which 8 were waited for; matrix products, arithmetic and copies ran while one was open for 14% of the time, Pallas kernels for 0%

profile of v1, /device:TPU:0, one launch (start us, length us, event | category | flops | bytes accessed | tf_op | source)
XLA Modules:
  0.0 418.9 jit_solution(17093387016553130761)
XLA Ops:
  7.2 0.7 all-gather.11.cloned.1.call-update
  8.0 0.7 all-gather.7.cloned.1.call-update
  8.7 0.7 all-gather.9.cloned.1.call-update
  10.0 12.3 %copy.52 = bf16[2048,2048]{0,1:T(8,128)(2,1)} copy(bf16[2048,2048]{1,0:T(8,128)(2,1)} %param.23) | data formatting | bytes 16777216 | tf_op args[6]
  22.4 6.2 %fusion.57 = (bf16[2048,1,8,128]{0,3,2,1:T(8,128)(2,1)}, bf16[2048,1,8,128]{0,3,2,1:T(8,128)(2,1)}) fusion(bf16[2048,2,8,128]{0,3,2,1:T(8,128)(2,1)} %bitcast.63), kind=kLoop, calls=%fused_computation.86 | loop fusion | bytes 16777216 | tf_op jit(solution)/shard_map/slice | solution.py:93
  28.5 6.5 %copy.60 = bf16[2048,1,8,128]{3,0,2,1:T(8,128)(2,1)} copy(bf16[2048,1,8,128]{0,3,2,1:T(8,128)(2,1)} %get-tuple-element.2) | data formatting | bytes 8388608
  35.0 6.7 %copy.61 = bf16[2048,1,8,128]{3,0,2,1:T(8,128)(2,1)} copy(bf16[2048,1,8,128]{0,3,2,1:T(8,128)(2,1)} %get-tuple-element.3) | data formatting | bytes 8388608
  42.7 20.8 %all-gather.11.cloned.1.call-done = bf16[2048,1024]{1,0:T(8,128)(2,1)} async-done(((bf16[128,1024]{1,0:T(8,128)(2,1)}), bf16[2048,1024]{1,0:T(8,128)(2,1)}) %all-gather.11.cloned.1.call-update) | async-done | bytes 4194320 | tf_op jit(solution)/shard_map/all_gather | solution.py:79
  63.5 3.1 convolution_convert_fusion.2
  66.6 48.1 %all-gather.7.cloned.1.call-done = bf16[2048,1024]{1,0:T(8,128)(2,1)} async-done(((bf16[128,1024]{1,0:T(8,128)(2,1)}), bf16[2048,1024]{1,0:T(8,128)(2,1)}) %all-gather.7.cloned.1.call-update) | async-done | bytes 4194320 | tf_op jit(solution)/shard_map/all_gather | solution.py:80
  114.7 3.1 convolution_convert_fusion.4
  117.8 48.1 %all-gather.9.cloned.1.call-done = bf16[2048,1024]{1,0:T(8,128)(2,1)} async-done(((bf16[128,1024]{1,0:T(8,128)(2,1)}), bf16[2048,1024]{1,0:T(8,128)(2,1)}) %all-gather.9.cloned.1.call-update) | async-done | bytes 4194320 | tf_op jit(solution)/shard_map/all_gather | solution.py:78
  166.0 3.2 fusion.22
  169.4 3.0 fusion.2
  172.5 4.4 %fusion.58 = f32[8,64]{1,0:T(8,128)S(1)} fusion(bf16[64,8,128]{2,0,1:T(8,128)(2,1)S(1)} %copy_bitcast_fusion.1, bf16[2048,8,128]{2,0,1:T(8,128)(2,1)} %bitcast.65, pred[64,2112]{1,0:T(8,128)(4,1)S(1)} %pad_add_fusion, bf16[8,8,8,128]{3,2,1,0:T(8,128)(2,1)S(1)} %fusion.22), kind=kOutput, calls=%fused_computation.87 | convolution fusion | flops 289802304 | bytes 4593664 | tf_op jit(solution)/shard_map/sub | solution.py:107
  176.8 6.1 %fusion.23 = bf16[8,8,8,128]{3,2,1,0:T(8,128)(2,1)S(1)} fusion(bf16[64,8,128]{2,0,1:T(8,128)(2,1)S(1)} %copy_bitcast_fusion, bf16[2048,8,128]{2,0,1:T(8,128)(2,1)} %bitcast.64, f32[8,64]{1,0:T(8,128)S(1)} %fusion.58, f32[8,64,2112]{2,1,0:T(8,128)} %fusion.2), kind=kOutput, calls=%fused_computation.28 | convolution fusion | flops 288787008 | bytes 8783872 | tf_op jit(solution)/shard_map/htr,rhc->thc/dot_general | solution.py:110
  183.0 34.1 %all-gather.13.cloned.1.call-done = bf16[2048,1024]{1,0:T(8,128)(2,1)} async-done(((bf16[128,1024]{1,0:T(8,128)(2,1)}), bf16[2048,1024]{1,0:T(8,128)(2,1)}) %all-gather.13.cloned.1.call-update) | async-done | bytes 4194320 | tf_op jit(solution)/shard_map/all_gather | solution.py:81
  217.1 4.3 %convolution_convert_fusion.1 = bf16[64,2048]{1,0:T(8,128)(2,1)} fusion(bf16[2048,1024]{1,0:T(8,128)(2,1)} %all-gather.13.cloned.1.call-done, bf16[8,8,8,128]{3,2,1,0:T(8,128)(2,1)S(1)} %fusion.23), kind=kOutput, calls=%fused_computation.16 | convolution fusion | flops 268566528 | bytes 4587520 | tf_op jit(solution)/shard_map/tc,dc->td/dot_general | solution.py:114
  221.4 21.8 %all-reduce.3.cloned.1.call-done = bf16[64,2048]{1,0:T(8,128)(2,1)} async-done(((bf16[64,2048]{1,0:T(8,128)(2,1)}), bf16[64,2048]{1,0:T(8,128)(2,1)}) %all-reduce.3.cloned.1.call-update) | async-done | bytes 262160 | tf_op jit(solution)/shard_map/psum | solution.py:115
  243.2 1.1 multiply_reduce_fusion
  244.4 1.8 multiply_convert_fusion.2
  246.3 22.1 %all-gather = f32[16,64,16]{1,2,0:T(8,128)S(1)} all-gather(f32[1,64,16]{1,2,0:T(8,128)S(1)} %bitcast.68), channel_id=1, replica_groups=mesh['dp'=2,'expert'=16] {'expert'}, dimensions={0}, use_global_device_ids=true | all-gather | bytes 69632 | tf_op jit(solution)/shard_map/all_gather | solution.py:133
  268.7 28.4 %all-gather.15.cloned.1.call-done = bf16[1024,2048]{1,0:T(8,128)(2,1)} async-done(((bf16[64,2048]{1,0:T(8,128)(2,1)}), bf16[1024,2048]{1,0:T(8,128)(2,1)}) %all-gather.15.cloned.1.call-update) | async-done | bytes 4194320 | tf_op jit(solution)/shard_map/all_gather | solution.py:134
  297.1 6.6 %fusion.13 = f32[1024,512]{1,0:T(8,128)} fusion(bf16[1024,2048]{1,0:T(8,128)(2,1)} %all-gather.15.cloned.1.call-done, bf16[1,2048,512]{2,1,0:T(8,128)(2,1)} %param.30), kind=kOutput, calls=%fused_computation.18 | convolution fusion | flops 2147483648 | bytes 8388608 | tf_op jit(solution)/shard_map/dot_general | solution.py:139
  303.6 10.1 %multiply_convert_fusion = bf16[1024,2048]{1,0:T(8,128)(2,1)} fusion(f32[1024]{0:T(1024)S(1)} %select_reduce_fusion, bf16[1,512,2048]{2,1,0:T(8,128)(2,1)S(1)} %copy-done, f32[1024,512]{1,0:T(8,128)} %fusion.13, bf16[1024,2048]{1,0:T(8,128)(2,1)} %all-gather.15.cloned.1.call-done, bf16[1,2048,512]{2,1,0:T(8,128)(2,1)} %param.29), kind=kOutput, calls=%fused_computation.1 | convolution fusion | flops 4306501632 | bytes 14684160 | tf_op jit(solution)/shard_map/dot_general | solution.py:141
  313.7 0.6 copy-done.11
  314.5 1.1 fusion.11
  315.6 3.6 all-to-all-start
  319.2 65.8 %reduce-scatter.2.cloned.1.call-done = bf16[64,2048]{1,0:T(8,128)(2,1)} async-done(((bf16[1024,2048]{1,0:T(8,128)(2,1)}), bf16[64,2048]{1,0:T(8,128)(2,1)}) %reduce-scatter.2.cloned.1.call-update) | async-done | bytes 262160 | tf_op jit(solution)/shard_map/reduce_scatter | solution.py:145
  385.1 24.4 %all-reduce.5.cloned.1.call-done = bf16[64,2048]{1,0:T(8,128)(2,1)} async-done(((bf16[64,2048]{1,0:T(8,128)(2,1)}), bf16[64,2048]{1,0:T(8,128)(2,1)}) %all-reduce.5.cloned.1.call-update) | async-done | bytes 262160 | tf_op jit(solution)/shard_map/psum | solution.py:148
  409.6 1.7 add_convert_fusion
  411.3 0.8 copy.83
  (59 shorter events, 2.6 us)
Async XLA Ops:
  7.2 296.5 %copy-start = (bf16[1,512,2048]{2,1,0:T(8,128)(2,1)S(1)}, bf16[1,512,2048]{2,1,0:T(8,128)(2,1)}, u32[]{:S(2)}) copy-start(bf16[1,512,2048]{2,1,0:T(8,128)(2,1)} %param.31) | copy-start | bytes 6291460
  7.2 56.3 %all-gather.11.cloned.1.call-start = ((), (), s32[]{:S(2)}) async-start(), calls=%async_computation.4 | async-start | bytes 4456448 | tf_op jit(solution)/shard_map/all_gather | solution.py:79
  7.9 106.8 %all-gather.7.cloned.1.call-start = ((), (), s32[]{:S(2)}) async-start(), calls=%async_computation.2 | async-start | bytes 4456448 | tf_op jit(solution)/shard_map/all_gather | solution.py:80
  8.7 157.3 %all-gather.9.cloned.1.call-start = ((), (), s32[]{:S(2)}) async-start(), calls=%async_computation.3 | async-start | bytes 4456448 | tf_op jit(solution)/shard_map/all_gather | solution.py:78
  9.4 207.7 %all-gather.13.cloned.1.call-start = ((), (), s32[]{:S(2)}) async-start(), calls=%async_computation.5 | async-start | bytes 4456448 | tf_op jit(solution)/shard_map/all_gather | solution.py:81
  10.0 233.3 %all-reduce.3.cloned.1.call-start = ((), (), s32[]{:S(2)}) async-start(), calls=%async_computation.6 | async-start | bytes 524288 | tf_op jit(solution)/shard_map/psum | solution.py:115
  35.0 6.7 %copy-start.9 = (s32[1,4]{1,0:T(1,128)S(1)}, s32[1,4]{1,0:T(1,128)}, u32[]{:S(2)}) copy-start(s32[1,4]{1,0:T(1,128)} %param.26) | copy-start | bytes 52
  35.0 6.8 %copy-start.10 = (s32[1,16]{1,0:T(1,128)S(1)}, s32[1,16]{1,0:T(1,128)}, u32[]{:S(2)}) copy-start(s32[1,16]{1,0:T(1,128)} %param.24) | copy-start | bytes 196
  35.0 7.1 %copy-start.8 = (s32[1,4]{1,0:T(1,128)S(1)}, s32[1,4]{1,0:T(1,128)}, u32[]{:S(2)}) copy-start(s32[1,4]{1,0:T(1,128)} %param.25) | copy-start | bytes 52
  35.0 7.2 %copy-start.1 = (bf16[64,2048]{1,0:T(8,128)(2,1)S(1)}, bf16[64,2048]{1,0:T(8,128)(2,1)}, u32[]{:S(2)}) copy-start(bf16[64,2048]{1,0:T(8,128)(2,1)} %param.17) | copy-start | bytes 786436
  35.0 28.4 %copy-start.4 = (f32[2048]{0:T(1024)S(1)}, f32[2048]{0:T(1024)}, u32[]{:S(2)}) copy-start(f32[2048]{0:T(1024)} %param.18) | copy-start | bytes 24580
  166.0 3.4 copy-start.2
  183.0 61.4 %copy-start.5 = (f32[2048]{0:T(1024)S(1)}, f32[2048]{0:T(1024)}, u32[]{:S(2)}) copy-start(f32[2048]{0:T(1024)} %param.28) | copy-start | bytes 24580
  183.0 63.3 %copy-start.6 = (f32[64,8]{0,1:T(8,128)S(1)}, f32[64,8]{0,1:T(8,128)}, u32[]{:S(2)}) copy-start(f32[64,8]{0,1:T(8,128)} %param.33) | copy-start | bytes 6148
  183.0 63.3 %copy-start.7 = (s32[64,8]{0,1:T(8,128)S(1)}, s32[64,8]{0,1:T(8,128)}, u32[]{:S(2)}) copy-start(s32[64,8]{0,1:T(8,128)} %param.32) | copy-start | bytes 6148
  221.4 75.7 %all-gather.15.cloned.1.call-start = ((), (), s32[]{:S(2)}) async-start(), calls=%async_computation.7 | async-start | bytes 4456448 | tf_op jit(solution)/shard_map/all_gather | solution.py:134
  246.2 138.9 %reduce-scatter.2.cloned.1.call-start = ((), (), s32[]{:S(2)}) async-start(), calls=%async_computation.8 | async-start | bytes 4456448 | tf_op jit(solution)/shard_map/reduce_scatter | solution.py:145
  313.7 0.7 copy-start.11
  313.7 95.9 %copy-start.3 = (bf16[64,2048]{1,0:T(8,128)(2,1)S(1)}, bf16[64,2048]{1,0:T(8,128)(2,1)}, u32[]{:S(2)}) copy-start(bf16[64,2048]{1,0:T(8,128)(2,1)} %all-reduce.3.cloned.1.call-done) | copy-start | bytes 786436
  315.6 69.5 %all-to-all-start = ((bf16[16,8,2048]{2,1,0:T(8,128)(2,1)}), bf16[16,8,2048]{2,1,0:T(8,128)(2,1)S(1)}, u32[]{:S(2)}, u32[]{:S(2)}) async-start(bf16[16,8,2048]{2,1,0:T(8,128)(2,1)} %fusion.11), calls=%async_computation.1 | async-start | bytes 1048576 | tf_op jit(solution)/shard_map/all_to_all | solution.py:130
  319.2 90.4 %all-reduce.5.cloned.1.call-start = ((), (), s32[]{:S(2)}) async-start(), calls=%async_computation.9 | async-start | bytes 524288 | tf_op jit(solution)/shard_map/psum | solution.py:148
Sparse Core Ops, SparseCore 0:
  10.2 53.2 all-gather.10
  65.6 49.0 all-gather.6
  116.9 49.0 all-gather.8
  168.0 49.0 all-gather.12
  221.5 21.6 all-reduce.2
  246.3 50.6 all-gather.14
  313.8 71.2 reduce-scatter.1
  387.4 22.1 all-reduce.4

commit v2 on v1

v2 whole, which is shorter than its diff:
```python
import functools

import jax
import jax.numpy as jnp
from jax import lax
from jax.experimental import pallas as pl
from jax.experimental.pallas import tpu as pltpu
from jax.sharding import PartitionSpec as P

HD = 128
PAGE = 128
VMEM_LIMIT = 56 * 1024 * 1024


EPSILON = 1e-05


def norm_rows(row_data, gain_vec):
    mean_sq = jnp.mean(row_data * row_data, axis=-1, keepdims=True)
    return (row_data * lax.rsqrt(mean_sq + EPSILON) * gain_vec).astype(jnp.bfloat16)


def owner_rank(owners):
    ids = jnp.arange(owners.shape[0], dtype=jnp.int32)
    same = (owners[:, None] == owners[None, :]) & (ids[None, :] < ids[:, None])
    return jnp.sum(same.astype(jnp.int32), axis=1)


def key_masks(table_row, cache_lens, new_lens, row_count, page_size):
    req_count = cache_lens.shape[0]
    pages_here = table_row.shape[0]
    per_request = pages_here // req_count
    slot_ids = jnp.arange(pages_here, dtype=jnp.int32)
    matches = (table_row[:, None] == slot_ids[None, :]).astype(jnp.int32)
    slot_of_page = jnp.sum(matches * slot_ids[:, None], axis=0)
    page_request = slot_of_page // per_request
    page_start = slot_of_page % per_request * page_size
    key_request = jnp.repeat(page_request, page_size)
    key_position = jnp.repeat(page_start, page_size) + jnp.tile(
        jnp.arange(page_size, dtype=jnp.int32), pages_here
    )
    request_ids = jnp.arange(req_count, dtype=jnp.int32)
    key_length = jnp.sum(
        (key_request[:, None] == request_ids[None, :]).astype(jnp.int32) * cache_lens[None, :],
        axis=1,
    )
    request_ends = jnp.sum(
        jnp.where(request_ids[None, :] <= request_ids[:, None], new_lens[None, :], 0), axis=1
    )
    tok_ids = jnp.arange(row_count, dtype=jnp.int32)
    tok_request = jnp.sum((tok_ids[:, None] >= request_ends[None, :]).astype(jnp.int32), axis=1)
    cached = (tok_request[:, None] == key_request[None, :]) & (key_position < key_length)[None, :]
    fresh_mask = tok_request[:, None] == tok_request[None, :]
    return jnp.concatenate([cached, fresh_mask], axis=1)


def grid_place(nx):
    me = lax.axis_index("expert")
    return me // (2 * nx), (me // 2) % nx, me % 2


def remote(src, dst, send_sem, recv_sem, device):
    return pltpu.make_async_remote_copy(
        src_ref=src,
        dst_ref=dst,
        send_sem=send_sem,
        recv_sem=recv_sem,
        device_id=device,
        device_id_type=pl.DeviceIdType.MESH,
    )


def greet(nz, nx, ndp, z, x, c):
    def index(z_to, x_to, c_to):
        return (lax.axis_index("dp"), (z_to * nx + x_to) * 2 + c_to)

    barrier = pltpu.get_barrier_semaphore()
    peers = [index(z, x, 1 - c)]
    peers += [index(z, (x + k) % nx, c) for k in range(1, nx)]
    peers += [index((z + k) % nz, x, c) for k in range(1, nz)]
    peers += [
        ((lax.axis_index("dp") + k) % ndp, lax.axis_index("expert")) for k in range(1, ndp)
    ]
    for peer in peers:
        pl.semaphore_signal(barrier, inc=1, device_id=peer, device_id_type=pl.DeviceIdType.MESH)
    pl.semaphore_wait(barrier, len(peers))
    return index


def dp_sum(ndp, ybuf, ysend, yrecv):
    mine = lax.axis_index("dp")
    expert = lax.axis_index("expert")
    copies = []
    for k in range(1, ndp):
        copy = remote(
            ybuf.at[mine],
            ybuf.at[mine],
            ysend.at[k - 1],
            yrecv.at[k - 1],
            ((mine + k) % ndp, expert),
        )
        copy.start()
        copies.append(copy)
    for copy in copies:
        copy.wait()
    total = ybuf[0].astype(jnp.float32)
    for d in range(1, ndp):
        total = total + ybuf[d].astype(jnp.float32)
    return total


def scatter_kernel(
    nz, nx, ndp, part, out, cbuf, xbuf, zbuf, ybuf,
    csend, crecv, xsend, xrecv, zsend, zrecv, ysend, yrecv,
):
    z, x, c = grid_place(nx)
    index = greet(nz, nx, ndp, z, x, c)

    def to_core(j, k):
        zz, xx = (z + j) % nz, (x + k) % nx
        return remote(
            part.at[zz, xx, 1 - c], cbuf.at[zz, xx], csend.at[j, k], crecv.at[j, k],
            index(z, x, 1 - c),
        )

    def to_x(j, k):
        zz, xx = (z + j) % nz, (x + k) % nx
        return remote(
            cbuf.at[zz, xx], xbuf.at[k - 1, zz], xsend.at[k - 1, j], xrecv.at[k - 1, j],
            index(z, xx, c),
        )

    def to_z(j):
        zz = (z + j) % nz
        return remote(
            cbuf.at[zz, x], zbuf.at[j - 1], zsend.at[j - 1], zrecv.at[j - 1], index(zz, x, c)
        )

    def order(i):
        return (i + 1) % nz

    def start_core(i, carry):
        for k in range(1, nx):
            to_core(order(i), k).start()
        return carry

    def start_own(i, carry):
        to_core(order(i), 0).start()
        return carry

    def x_step(i, carry):
        j = order(i)
        zz = (z + j) % nz
        for k in range(1, nx):
            xx = (x + k) % nx
            to_core(j, k).wait_recv()
            summed = cbuf[zz, xx].astype(jnp.float32) + part[zz, xx, c].astype(jnp.float32)
            cbuf[zz, xx] = summed.astype(jnp.bfloat16)
            to_x(j, k).start()
        return carry

    def column(j):
        zz = (z + j) % nz
        to_core(j, 0).wait_recv()
        summed = cbuf[zz, x].astype(jnp.float32) + part[zz, x, c].astype(jnp.float32)
        for k in range(1, nx):
            to_x(j, k).wait_recv()
            summed = summed + xbuf[k - 1, zz].astype(jnp.float32)
        return zz, summed

    def z_step(j, carry):
        zz, summed = column(j)
        cbuf[zz, x] = summed.astype(jnp.bfloat16)
        to_z(j).start()
        return carry

    lax.fori_loop(0, nz, start_core, 0)
    lax.fori_loop(0, nz, start_own, 0)
    lax.fori_loop(0, nz, x_step, 0)
    lax.fori_loop(1, nz, z_step, 0)
    _, total = column(0)
    for j in range(1, nz):
        to_z(j).wait_recv()
        total = total + zbuf[j - 1].astype(jnp.float32)
    if ndp > 1:
        ybuf[lax.axis_index("dp")] = total.astype(jnp.bfloat16)
        total = dp_sum(ndp, ybuf, ysend, yrecv)
    out[...] = total.astype(out.dtype)

    def drain(j, carry):
        for k in range(nx):
            to_core(j, k).wait_send()
        for k in range(1, nx):
            to_x(j, k).wait_send()
        return carry

    lax.fori_loop(0, nz, drain, 0)
    for j in range(1, nz):
        to_z(j).wait_send()


def scatter_sum(part, nz, nx, ndp, dtype, collective_id):
    rows, cols = part.shape[0] // (nz * nx * 2), part.shape[1]
    block = (rows, cols)
    dma = pltpu.SemaphoreType.DMA
    spread = max(1, ndp - 1)
    return pl.pallas_call(
        functools.partial(scatter_kernel, nz, nx, ndp),
        out_shape=jax.ShapeDtypeStruct(block, dtype),
        in_specs=[pl.BlockSpec(memory_space=pltpu.VMEM)],
        out_specs=pl.BlockSpec(memory_space=pltpu.VMEM),
        scratch_shapes=[
            pltpu.VMEM((nz, nx) + block, jnp.bfloat16),
            pltpu.VMEM((nx - 1, nz) + block, jnp.bfloat16),
            pltpu.VMEM((nz - 1,) + block, jnp.bfloat16),
            pltpu.VMEM((ndp,) + block, jnp.bfloat16),
            dma((nz, nx)), dma((nz, nx)),
            dma((nx - 1, nz)), dma((nx - 1, nz)),
            dma((nz - 1,)), dma((nz - 1,)),
            dma((spread,)), dma((spread,)),
        ],
        compiler_params=pltpu.CompilerParams(
            collective_id=collective_id, has_side_effects=True, vmem_limit_bytes=VMEM_LIMIT
        ),
    )(part.reshape((nz, nx, 2) + block))


def gather_kernel(
    nz, nx, ndp, attn, tokens, gain, extra, out, residual, own, ybuf,
    ysend, yrecv, zsend, zrecv, xsend, xrecv, csend, crecv, local_sem,
):
    z, x, c = grid_place(nx)
    index = greet(nz, nx, ndp, z, x, c)
    width = tokens.shape[1]
    ybuf[lax.axis_index("dp")] = attn[...]
    resid = tokens[...].astype(jnp.float32) + dp_sum(ndp, ybuf, ysend, yrecv)
    residual[...] = resid
    own[:, :width] = norm_rows(resid, gain[...])
    own[:, width:] = extra[...]

    def block(j, k):
        return out.at[(z + nz - j) % nz, (x + nx - k) % nx, c]

    def to_z(j):
        return remote(own, out.at[z, x, c], zsend.at[j - 1], zrecv.at[j - 1], index((z + j) % nz, x, c))

    def to_x(src, j, k):
        return remote(
            src, block(j, 0), xsend.at[j, k - 1], xrecv.at[j, k - 1], index(z, (x + k) % nx, c)
        )

    def to_core(src, j, k):
        return remote(src, block(j, k), csend.at[j, k], crecv.at[j, k], index(z, x, 1 - c))

    keep = pltpu.make_async_copy(own, out.at[z, x, c], local_sem)
    keep.start()
    for j in range(1, nz):
        to_z(j).start()
    for k in range(1, nx):
        to_x(own, 0, k).start()
    to_core(own, 0, 0).start()

    def z_step(j, carry):
        to_z(j).wait_recv()
        for k in range(1, nx):
            to_x(block(j, 0), j, k).start()
        to_core(block(j, 0), j, 0).start()
        return carry

    def x_step(j, carry):
        for k in range(1, nx):
            to_x(own, j, k).wait_recv()
            to_core(block(j, k), j, k).start()
        return carry

    def core_step(j, carry):
        for k in range(nx):
            to_core(own, j, k).wait_recv()
        for k in range(nx):
            to_core(own, j, k).wait_send()
        for k in range(1, nx):
            to_x(own, j, k).wait_send()
        return carry

    lax.fori_loop(1, nz, z_step, 0)
    lax.fori_loop(0, nz, x_step, 0)
    lax.fori_loop(0, nz, core_step, 0)
    for j in range(1, nz):
        to_z(j).wait_send()
    keep.wait()


def gather_normed(attn, tokens, gain, extra, nz, nx, ndp, collective_id):
    rows, width = tokens.shape
    cols = width + extra.shape[1]
    dma = pltpu.SemaphoreType.DMA
    whole = pl.BlockSpec(memory_space=pltpu.VMEM)
    out, residual = pl.pallas_call(
        functools.partial(gather_kernel, nz, nx, ndp),
        out_shape=(
            jax.ShapeDtypeStruct((nz, nx, 2, rows, cols), jnp.bfloat16),
            jax.ShapeDtypeStruct((rows, width), jnp.float32),
        ),
        in_specs=[whole] * 4,
        out_specs=(pl.BlockSpec(memory_space=pl.ANY), whole),
        scratch_shapes=[
            pltpu.VMEM((rows, cols), jnp.bfloat16),
            pltpu.VMEM((ndp, rows, width), jnp.bfloat16),
            dma((ndp - 1,)), dma((ndp - 1,)),
            dma((nz - 1,)), dma((nz - 1,)),
            dma((nz, nx - 1)), dma((nz, nx - 1)),
            dma((nz, nx)), dma((nz, nx)),
            dma,
        ],
        compiler_params=pltpu.CompilerParams(
            collective_id=collective_id, has_side_effects=True, vmem_limit_bytes=VMEM_LIMIT
        ),
    )(attn, tokens, gain.reshape(1, width), extra)
    return out.reshape(nz * nx * 2 * rows, cols), residual


def attention_kernel(query, new_key, new_value, key, value, mask, fresh_mask, out):
    def scored(keys, valid):
        scores = lax.dot_general(
            query[...], keys, (((1,), (1,)), ((), ())), preferred_element_type=jnp.float32
        ) * HD ** (-0.5)
        return jnp.where(valid > 0, scores, -1e30)

    old = scored(key[...], mask[...])
    new = scored(new_key[...], fresh_mask[...])
    highest = jnp.maximum(
        jnp.max(old, axis=-1, keepdims=True), jnp.max(new, axis=-1, keepdims=True)
    )
    old, new = jnp.exp(old - highest), jnp.exp(new - highest)
    total = jnp.sum(old, axis=-1, keepdims=True) + jnp.sum(new, axis=-1, keepdims=True)
    old, new = (old / total).astype(jnp.bfloat16), (new / total).astype(jnp.bfloat16)
    out[...] = (
        jnp.dot(old, value[...], preferred_element_type=jnp.float32)
        + jnp.dot(new, new_value[...], preferred_element_type=jnp.float32)
    ).astype(jnp.bfloat16)


def attention(qkv, cache, valid, heads):
    rows, kept = qkv.shape[0], cache.shape[0]

    def columns(count, first):
        return pl.BlockSpec((count, HD), lambda h: (0, first + h))

    def fixed(width):
        return pl.BlockSpec((rows, width), lambda h: (0, 0))

    return pl.pallas_call(
        attention_kernel,
        grid=(heads,),
        out_shape=jax.ShapeDtypeStruct((rows, heads * HD), jnp.bfloat16),
        in_specs=[
            columns(rows, 0), columns(rows, heads), columns(rows, 2 * heads),
            columns(kept, 0), columns(kept, heads), fixed(kept), fixed(rows),
        ],
        out_specs=columns(rows, 0),
        compiler_params=pltpu.CompilerParams(vmem_limit_bytes=VMEM_LIMIT),
    )(qkv, qkv, qkv, cache, cache, valid[:, :kept], valid[:, kept:])


def in_pieces(values):
    pieces = []
    for _ in range(3):
        top = lax.reduce_precision(values, 8, 7)
        pieces.append(top.astype(jnp.bfloat16))
        values = values - top
    return pieces


def local(
    tokens,
    attn_gain,
    w_query,
    w_key,
    w_value,
    w_out,
    cache,
    page_table,
    cache_len,
    new_len,
    kv_owner,
    moe_gain,
    w_gate,
    w_up,
    w_down,
    expert_ids,
    gate_weights,
):
    row_count, model_width = tokens.shape
    n_expert, ndp = lax.axis_size("expert"), lax.axis_size("dp")
    nx, nz = ndp, n_expert // (2 * ndp)
    local_experts = w_gate.shape[0]
    experts_all = n_expert * local_experts
    kv_cap = max(2, 2 * row_count // n_expert)
    heads = w_query.shape[1] // HD
    depth = w_query.shape[0]
    full_out = lax.all_gather(w_out, "expert", axis=0, tiled=True)
    normed = norm_rows(tokens.astype(jnp.float32), attn_gain)
    strips = normed.reshape(row_count, n_expert, depth).transpose(1, 0, 2)
    strips = lax.all_to_all(strips, "expert", split_axis=0, concat_axis=0, tiled=True)
    strips = strips.reshape(n_expert * row_count, depth)
    terms = jnp.dot(
        strips,
        jnp.concatenate([w_query, w_key, w_value], axis=1),
        preferred_element_type=jnp.float32,
    ).astype(jnp.bfloat16)
    qkv = scatter_sum(terms, nz, nx, 1, jnp.bfloat16, 1)
    valid = key_masks(page_table[0], cache_len[0], new_len[0], row_count, PAGE)
    heads_out = attention(qkv, cache, valid.astype(jnp.int32), heads)
    attn_part = jnp.einsum(
        "tc,dc->td", heads_out, full_out, preferred_element_type=jnp.float32
    ).astype(jnp.bfloat16)
    labels = jnp.arange(experts_all, dtype=jnp.int32)
    gates = jnp.sum(
        jnp.where(expert_ids[:, :, None] == labels, gate_weights[:, :, None], 0.0), axis=1
    )
    extra = jnp.concatenate(in_pieces(gates), axis=1)
    extra = jnp.pad(extra, ((0, 0), (0, -extra.shape[1] % 128)))
    packed, residual = gather_normed(attn_part, tokens, moe_gain, extra, nz, nx, ndp, 2)
    kv_row = qkv[:, heads * HD :]
    kv_slot = kv_owner[:, 0] * kv_cap + owner_rank(kv_owner[:, 0])
    slots = jnp.arange(n_expert * kv_cap, dtype=jnp.int32)
    kv_buffer = jnp.dot(
        (slots[:, None] == kv_slot[None, :]).astype(jnp.bfloat16),
        kv_row,
        preferred_element_type=jnp.float32,
    ).astype(jnp.bfloat16)
    new_rows = lax.all_to_all(
        kv_buffer.reshape(n_expert, kv_cap, -1), "expert", split_axis=0, concat_axis=0, tiled=True
    ).reshape(n_expert * kv_cap, -1)
    rows = packed[:, :model_width]
    all_gates = packed[:, model_width : model_width + 3 * experts_all].astype(jnp.float32)
    all_gates = all_gates.reshape(-1, 3, experts_all)
    all_gates = all_gates[:, 0] + (all_gates[:, 1] + all_gates[:, 2])
    first = lax.axis_index("expert") * local_experts
    gated = 0.0
    for local_id in range(local_experts):
        gate_proj = jnp.dot(rows, w_gate[local_id], preferred_element_type=jnp.float32)
        up_proj = jnp.dot(rows, w_up[local_id], preferred_element_type=jnp.float32)
        active = (jax.nn.silu(gate_proj) * up_proj).astype(jnp.bfloat16)
        part = jnp.dot(active, w_down[local_id], preferred_element_type=jnp.float32)
        part = part.astype(jnp.bfloat16).astype(jnp.float32)
        mine = jnp.sum(jnp.where(labels == first + local_id, all_gates, 0.0), axis=1)
        gated = gated + part * mine[:, None]
    moe_total = scatter_sum(gated.astype(jnp.bfloat16), nz, nx, ndp, jnp.float32, 3)
    out = (residual + moe_total).astype(jnp.bfloat16)
    return (out, new_rows)


def solution(mesh):
    placed = (
        P("expert", None),
        P(),
        P("expert", "dp"),
        P("expert", "dp"),
        P("expert", "dp"),
        P("expert", "dp"),
        P("expert", "dp"),
        P("expert", None),
        P("expert", None),
        P("expert", None),
        P("expert", None),
        P(),
        P("expert", None, "dp"),
        P("expert", None, "dp"),
        P("expert", "dp", None),
        P("expert", None),
        P("expert", None),
    )
    return jax.shard_map(
        local,
        mesh=mesh,
        in_specs=placed,
        out_specs=(P("expert", None), P("expert", "dp")),
        check_vma=False,
    )
```

time: 420 us -> 256 us (0.61)
  waiting for transfers between devices: 294 us -> 13.7 us
  Pallas kernels: 0 us -> 172 us
  local copies, waits for them, and re-layouts: 33.6 us -> 3.81 us
  blocking collectives: 22.1 us -> 0 us
  matrix products: 44.9 us -> 27.4 us
  starting transfers between devices: 3.89 us -> 17.8 us
    all_gather x5 -> x1, waiting for transfers between devices: 179 us -> 0.01 us  [local(): full_out = lax.all_gather(w_out, 'expert', axis=0, tiled=True)]
    pallas_call x0 -> x4, Pallas kernels: none -> 172 us  [the longest x2 117 us: scatter_sum(): pl.pallas_call(functools.partial(scatter_kernel, nz, nx, ndp), out_shape=...]
    reduce_scatter x1 -> x0, waiting for transfers between devices: 65.8 us -> none  [local(): lax.psum_scatter(gated.astype(jnp.bfloat16), 'expert', scatter_dimension=...]
    psum x2 -> x0, waiting for transfers between devices: 46.2 us -> none  [the longest x1 24.4 us: local(): moe_total = lax.psum(moe_part, 'dp').astype(jnp.float32)]
    unnamed x29 -> x25, local copies, waits for them, and re-layouts: 27.3 us -> 1 us
    all_gather x1 -> x0, blocking collectives: 22.1 us -> none  [local(): all_gates = lax.all_gather(gates, 'expert', axis=0, tiled=True)]
    dot_general x6 -> x2, matrix products: 25.1 us -> 11 us  [the longest x1 6.56 us: local(): jnp.dot(rows, w_gate[local_id], preferred_element_type=jnp.float32)]
    all_to_all x0 -> x1, waiting for transfers between devices: none -> 11.2 us  [local(): lax.all_to_all(strips, 'expert', split_axis=0, concat_axis=0, tiled=True)]
  transfers between devices with their start and end apart: 9 -> 3, of which waited for: 8 -> 2; matrix products, arithmetic and copies ran while one was open for 14% -> 5% of each run, Pallas kernels for 0% -> 29%
where the time goes in v2:
time: 256 us
  Pallas kernels  172 us (67%)
  matrix products  27.4 us (11%)
  starting transfers between devices  17.8 us (7%)
  between operations  14.3 us (6%)
  waiting for transfers between devices  13.7 us (5%)
  other arithmetic  6.41 us (3%)
  local copies, waits for them, and re-layouts  3.81 us (1%)
    pallas_call x2, Pallas kernels, scatter_sum(): pl.pallas_call(functools.partial(scatter_kernel, nz, nx, ndp), out_shape=...  117 us
    pallas_call x1, Pallas kernels, gather_normed(): pl.pallas_call(functools.partial(gather_kernel, nz, nx, ndp), out_shape=(...  45.5 us
    all_to_all x1, waiting for transfers between devices, local(): lax.all_to_all(strips, 'expert', split_axis=0, concat_axis=0, tiled=True)  11.2 us
    all_to_all x1, starting transfers between devices, local(): lax.all_to_all(kv_buffer.reshape(n_expert, kv_cap, -1), 'expert', split_a...  10.4 us
    pallas_call x1, Pallas kernels, attention(): pl.pallas_call(attention_kernel, grid=(heads,), out_shape=jax.ShapeDtypeS...  10.2 us
    dot_general x1, matrix products, local(): part = jnp.dot(active, w_down[local_id], preferred_element_type=jnp.float32)  10 us
    all_to_all x1, starting transfers between devices, local(): lax.all_to_all(strips, 'expert', split_axis=0, concat_axis=0, tiled=True)  7.36 us
    dot_general x1, matrix products, local(): jnp.dot(rows, w_gate[local_id], preferred_element_type=jnp.float32)  6.56 us
  transfers between devices with their start and end apart: 3, of which 2 were waited for; matrix products, arithmetic and copies ran while one was open for 5% of the time, Pallas kernels for 29%

profile of v2, /device:TPU:0, one launch (start us, length us, event | category | flops | bytes accessed | tf_op | source)
XLA Modules:
  0.0 255.5 jit_solution(3491552347271721461)
XLA Ops:
  7.3 0.7 all-gather.2.cloned.1.call-update
  8.0 1.1 fusion.21
  9.1 1.1 fusion.24
  10.3 0.8 copy.36
  11.1 7.4 %all-to-all-start = ((bf16[16,64,128]{2,1,0:T(8,128)(2,1)}), bf16[16,64,128]{2,1,0:T(8,128)(2,1)S(1)}, u32[]{:S(2)}, u32[]{:S(2)}) async-start(bf16[16,64,128]{2,1,0:T(8,128)(2,1)} %copy.36), calls=%async_computation | async-start | bytes 524288 | tf_op jit(solution)/shard_map/all_to_all | solution.py:404
  18.4 0.1 select_reduce_fusion.3
  18.6 0.1 convert_reduce_fusion.1
  18.6 0.1 select_reduce_fusion.2
  18.7 0.2 convert_reduce_fusion
  19.0 0.1 select_reduce_fusion.1
  19.3 0.2 compare_and_fusion
  19.4 11.2 %all-to-all-done = bf16[16,64,128]{2,1,0:T(8,128)(2,1)S(1)} async-done(((bf16[16,64,128]{2,1,0:T(8,128)(2,1)}), bf16[16,64,128]{2,1,0:T(8,128)(2,1)S(1)}, u32[]{:S(2)}, u32[]{:S(2)}) %all-to-all-start) | async-done | bytes 262176 | tf_op jit(solution)/shard_map/all_to_all | solution.py:404
  30.6 4.4 %convolution_convert_fusion = bf16[1024,3072]{1,0:T(8,128)(2,1)} fusion(bf16[1024,128]{1,0:T(8,128)(2,1)S(1)} %bitcast.49, bf16[128,1024]{1,0:T(8,128)(2,1)S(1)} %copy-done.2, bf16[128,1024]{1,0:T(8,128)(2,1)S(1)} %copy-done.3, bf16[128,1024]{1,0:T(8,128)(2,1)S(1)} %copy-done.4), kind=kOutput, calls=%fused_computation.1 | convolution fusion | flops 810811392 | bytes 7340032 | tf_op jit(solution)/shard_map/dot_general | solution.py:406
  35.1 63.5 %shard_map.176.query.new_key.new_value = bf16[64,3072]{1,0:T(8,128)(2,1)} custom-call(bf16[4,2,2,64,3072]{4,3,2,1,0:T(8,128)(2,1)} %bitcast.46), custom_call_target="tpu_custom_call" | custom-call | tf_op jit(solution)/shard_map/pallas_call | solution.py:207
  98.5 2.0 fusion.4
  100.6 10.4 %all-to-all-start.1 = ((bf16[16,8,2048]{2,1,0:T(8,128)(2,1)}), bf16[16,8,2048]{2,1,0:T(8,128)(2,1)S(1)}, u32[]{:S(2)}, u32[]{:S(2)}) async-start(bf16[16,8,2048]{2,1,0:T(8,128)(2,1)} %fusion.4), calls=%async_computation.1 | async-start | bytes 1048576 | tf_op jit(solution)/shard_map/all_to_all | solution.py:432
  111.0 0.1 copy.38
  111.1 0.8 slice.32.mask
  112.0 0.7 fusion.38.extra
  112.7 0.6 add_convert_fusion.2.fresh_mask
  113.4 10.2 %shard_map.177 = bf16[64,1024]{1,0:T(8,128)(2,1)} custom-call(bf16[64,3072]{1,0:T(8,128)(2,1)} %shard_map.176.query.new_key.new_value, bf16[64,3072]{1,0:T(8,128)(2,1)} %shard_map.176.query.new_key.new_value, bf16[64,3072]{1,0:T(8,128)(2,1)} %shard_map.176.query.new_key.new_value, bf16[2048,2048]{1,0:T(8,128)(2,1)} %value.1, bf16[2048,2048]{1,0:T(8,128)(2,1)} %value.1, ...), custom_call_target="tpu_custom_call" | custom-call | tf_op jit(solution)/shard_map/pallas_call | solution.py:352
  123.6 1.8 all-to-all-done.1
  125.4 4.4 %convolution_convert_fusion.2.attn = bf16[64,2048]{1,0:T(8,128)(2,1)} fusion(bf16[64,1024]{1,0:T(8,128)(2,1)} %shard_map.177, bf16[2048,1024]{1,0:T(8,128)(2,1)} %all-gather.2.cloned.1.call-done), kind=kOutput, calls=%fused_computation.8 | convolution fusion | flops 268566528 | bytes 4587520 | tf_op jit(solution)/shard_map/tc,dc->td/dot_general | solution.py:414
  129.8 45.5 %shard_map.178 = (bf16[4,2,2,64,2176]{4,3,2,1,0:T(8,128)(2,1)}, f32[64,2048]{1,0:T(8,128)}) custom-call(bf16[64,2048]{1,0:T(8,128)(2,1)} %convolution_convert_fusion.2.attn, bf16[64,2048]{1,0:T(8,128)(2,1)} %tokens.1, f32[1,2048]{1,0:T(1,128)} %bitcast.55, bf16[64,128]{1,0:T(8,128)(2,1)} %fusion.38.extra), custom_call_target="tpu_custom_call" | custom-call | tf_op jit(solution)/shard_map/pallas_call | solution.py:298
  175.2 1.0 slice.34
  176.2 0.1 copy.41
  176.4 6.6 %fusion.2 = f32[1024,512]{1,0:T(8,128)} fusion(bf16[1024,2176]{1,0:T(8,128)(2,1)} %bitcast.53, bf16[1,2048,512]{2,1,0:T(8,128)(2,1)} %param.29), kind=kOutput, calls=%fused_computation.4 | convolution fusion | flops 2147483648 | bytes 8388608 | tf_op jit(solution)/shard_map/dot_general | solution.py:442
  182.9 0.1 fusion.29
  183.0 10.0 %multiply_convert_fusion = bf16[1024,2048]{1,0:T(8,128)(2,1)} fusion(f32[1024]{0:T(1024)S(1)} %fusion.29, bf16[1,512,2048]{2,1,0:T(8,128)(2,1)S(1)} %copy-done, f32[1024,512]{1,0:T(8,128)} %fusion.2, bf16[1,2048,512]{2,1,0:T(8,128)(2,1)} %param.30, bf16[1024,2176]{1,0:T(8,128)(2,1)} %bitcast.54), kind=kOutput, calls=%fused_computation | convolution fusion | flops 4306501632 | bytes 14684160 | tf_op jit(solution)/shard_map/dot_general | solution.py:445
  193.0 53.0 %shard_map.179 = f32[64,2048]{1,0:T(8,128)} custom-call(bf16[4,2,2,64,2048]{4,3,2,1,0:T(8,128)(2,1)} %bitcast.47), custom_call_target="tpu_custom_call" | custom-call | tf_op jit(solution)/shard_map/pallas_call | solution.py:207
  246.1 1.8 add_convert_fusion.1
  247.9 0.8 copy.44
  (38 shorter events, 0.5 us)
Async XLA Ops:
  7.2 175.8 %copy-start = (bf16[1,512,2048]{2,1,0:T(8,128)(2,1)S(1)}, bf16[1,512,2048]{2,1,0:T(8,128)(2,1)}, u32[]{:S(2)}) copy-start(bf16[1,512,2048]{2,1,0:T(8,128)(2,1)} %param.31) | copy-start | bytes 6291460
  7.2 11.2 %copy-start.8 = (s32[1,4]{1,0:T(1,128)S(1)}, s32[1,4]{1,0:T(1,128)}, u32[]{:S(2)}) copy-start(s32[1,4]{1,0:T(1,128)} %param.26) | copy-start | bytes 52
  7.2 11.5 %copy-start.9 = (s32[1,16]{1,0:T(1,128)S(1)}, s32[1,16]{1,0:T(1,128)}, u32[]{:S(2)}) copy-start(s32[1,16]{1,0:T(1,128)} %param.24) | copy-start | bytes 196
  7.2 11.5 %copy-start.10 = (s32[64,1]{0,1:T(1,128)S(1)}, s32[64,1]{0,1:T(1,128)}, u32[]{:S(2)}) copy-start(s32[64,1]{0,1:T(1,128)} %param.27) | copy-start | bytes 772
  7.2 11.8 %copy-start.7 = (s32[1,4]{1,0:T(1,128)S(1)}, s32[1,4]{1,0:T(1,128)}, u32[]{:S(2)}) copy-start(s32[1,4]{1,0:T(1,128)} %param.25) | copy-start | bytes 52
  7.2 23.4 %copy-start.2 = (bf16[128,1024]{1,0:T(8,128)(2,1)S(1)}, bf16[128,1024]{1,0:T(8,128)(2,1)}, u32[]{:S(2)}) copy-start(bf16[128,1024]{1,0:T(8,128)(2,1)} %param.21) | copy-start | bytes 786436
  7.2 23.4 %copy-start.3 = (bf16[128,1024]{1,0:T(8,128)(2,1)S(1)}, bf16[128,1024]{1,0:T(8,128)(2,1)}, u32[]{:S(2)}) copy-start(bf16[128,1024]{1,0:T(8,128)(2,1)} %param.20) | copy-start | bytes 786436
  7.2 23.4 %copy-start.4 = (bf16[128,1024]{1,0:T(8,128)(2,1)S(1)}, bf16[128,1024]{1,0:T(8,128)(2,1)}, u32[]{:S(2)}) copy-start(bf16[128,1024]{1,0:T(8,128)(2,1)} %param.19) | copy-start | bytes 786436
  7.3 118.1 %all-gather.2.cloned.1.call-start = ((), (), s32[]{:S(2)}) async-start(), calls=%async_computation.2 | async-start | bytes 4456448 | tf_op jit(solution)/shard_map/all_gather | solution.py:401
  11.1 19.5 %all-to-all-start = ((bf16[16,64,128]{2,1,0:T(8,128)(2,1)}), bf16[16,64,128]{2,1,0:T(8,128)(2,1)S(1)}, u32[]{:S(2)}, u32[]{:S(2)}) async-start(bf16[16,64,128]{2,1,0:T(8,128)(2,1)} %copy.36), calls=%async_computation | async-start | bytes 524288 | tf_op jit(solution)/shard_map/all_to_all | solution.py:404
  35.1 75.9 %copy-start.5 = (f32[64,8]{0,1:T(8,128)S(1)}, f32[64,8]{0,1:T(8,128)}, u32[]{:S(2)}) copy-start(f32[64,8]{0,1:T(8,128)} %param.33) | copy-start | bytes 6148
  35.1 75.9 %copy-start.6 = (s32[64,8]{0,1:T(8,128)S(1)}, s32[64,8]{0,1:T(8,128)}, u32[]{:S(2)}) copy-start(s32[64,8]{0,1:T(8,128)} %param.32) | copy-start | bytes 6148
  100.6 24.8 %all-to-all-start.1 = ((bf16[16,8,2048]{2,1,0:T(8,128)(2,1)}), bf16[16,8,2048]{2,1,0:T(8,128)(2,1)S(1)}, u32[]{:S(2)}, u32[]{:S(2)}) async-start(bf16[16,8,2048]{2,1,0:T(8,128)(2,1)} %fusion.4), calls=%async_computation.1 | async-start | bytes 1048576 | tf_op jit(solution)/shard_map/all_to_all | solution.py:432
  193.0 53.1 %copy-start.1 = (f32[64,2048]{1,0:T(8,128)S(1)}, f32[64,2048]{1,0:T(8,128)}, u32[]{:S(2)}) copy-start(f32[64,2048]{1,0:T(8,128)} %get-tuple-element.4) | copy-start | bytes 1572868
Sparse Core Ops, SparseCore 0:
  10.2 77.5 all-gather.1

commit v3 on v2

--- a/solution.py
+++ b/solution.py
@@ -302,7 +302,7 @@
             jax.ShapeDtypeStruct((rows, width), jnp.float32),
         ),
         in_specs=[whole] * 4,
-        out_specs=(pl.BlockSpec(memory_space=pl.ANY), whole),
+        out_specs=(whole, whole),
         scratch_shapes=[
             pltpu.VMEM((rows, cols), jnp.bfloat16),
             pltpu.VMEM((ndp, rows, width), jnp.bfloat16),

time: 256 us -> 257 us (level)
  no operation moved by 1% of the time
where the time goes in v3:
time: 257 us; the launch traced here: 256 us
  Pallas kernels  173 us (67%)
  matrix products  27.4 us (11%)
  starting transfers between devices  17.8 us (7%)
  between operations  14.3 us (6%)
  waiting for transfers between devices  13.7 us (5%)
  other arithmetic  6.41 us (2%)
  local copies, waits for them, and re-layouts  3.81 us (1%)
    pallas_call x2, Pallas kernels, scatter_sum(): pl.pallas_call(functools.partial(scatter_kernel, nz, nx, ndp), out_shape=...  116 us
    pallas_call x1, Pallas kernels, gather_normed(): pl.pallas_call(functools.partial(gather_kernel, nz, nx, ndp), out_shape=(...  46.2 us
    all_to_all x1, waiting for transfers between devices, local(): lax.all_to_all(strips, 'expert', split_axis=0, concat_axis=0, tiled=True)  11.2 us
    all_to_all x1, starting transfers between devices, local(): lax.all_to_all(kv_buffer.reshape(n_expert, kv_cap, -1), 'expert', split_a...  10.4 us
    pallas_call x1, Pallas kernels, attention(): pl.pallas_call(attention_kernel, grid=(heads,), out_shape=jax.ShapeDtypeS...  10.2 us
    dot_general x1, matrix products, local(): part = jnp.dot(active, w_down[local_id], preferred_element_type=jnp.float32)  10 us
    all_to_all x1, starting transfers between devices, local(): lax.all_to_all(strips, 'expert', split_axis=0, concat_axis=0, tiled=True)  7.36 us
    dot_general x1, matrix products, local(): jnp.dot(rows, w_gate[local_id], preferred_element_type=jnp.float32)  6.56 us
  transfers between devices with their start and end apart: 3, of which 2 were waited for; matrix products, arithmetic and copies ran while one was open for 5% of the time, Pallas kernels for 29%

profile of v3, /device:TPU:0, one launch (start us, length us, event | category | flops | bytes accessed | tf_op | source)
XLA Modules:
  0.0 256.2 jit_solution(13596675462102416273)
XLA Ops:
  7.3 0.7 all-gather.2.cloned.1.call-update
  8.0 1.1 fusion.21
  9.1 1.1 fusion.24
  10.3 0.8 copy.36
  11.1 7.4 %all-to-all-start = ((bf16[16,64,128]{2,1,0:T(8,128)(2,1)}), bf16[16,64,128]{2,1,0:T(8,128)(2,1)S(1)}, u32[]{:S(2)}, u32[]{:S(2)}) async-start(bf16[16,64,128]{2,1,0:T(8,128)(2,1)} %copy.36), calls=%async_computation | async-start | bytes 524288 | tf_op jit(solution)/shard_map/all_to_all | solution.py:404
  18.4 0.1 select_reduce_fusion.3
  18.6 0.1 convert_reduce_fusion.1
  18.6 0.1 select_reduce_fusion.2
  18.7 0.2 convert_reduce_fusion
  19.0 0.1 select_reduce_fusion.1
  19.3 0.2 compare_and_fusion
  19.4 11.2 %all-to-all-done = bf16[16,64,128]{2,1,0:T(8,128)(2,1)S(1)} async-done(((bf16[16,64,128]{2,1,0:T(8,128)(2,1)}), bf16[16,64,128]{2,1,0:T(8,128)(2,1)S(1)}, u32[]{:S(2)}, u32[]{:S(2)}) %all-to-all-start) | async-done | bytes 262176 | tf_op jit(solution)/shard_map/all_to_all | solution.py:404
  30.6 4.4 %convolution_convert_fusion = bf16[1024,3072]{1,0:T(8,128)(2,1)} fusion(bf16[1024,128]{1,0:T(8,128)(2,1)S(1)} %bitcast.49, bf16[128,1024]{1,0:T(8,128)(2,1)S(1)} %copy-done.2, bf16[128,1024]{1,0:T(8,128)(2,1)S(1)} %copy-done.3, bf16[128,1024]{1,0:T(8,128)(2,1)S(1)} %copy-done.4), kind=kOutput, calls=%fused_computation.1 | convolution fusion | flops 810811392 | bytes 7340032 | tf_op jit(solution)/shard_map/dot_general | solution.py:406
  35.1 63.5 %shard_map.176.query.new_key.new_value = bf16[64,3072]{1,0:T(8,128)(2,1)} custom-call(bf16[4,2,2,64,3072]{4,3,2,1,0:T(8,128)(2,1)} %bitcast.46), custom_call_target="tpu_custom_call" | custom-call | tf_op jit(solution)/shard_map/pallas_call | solution.py:207
  98.5 2.0 fusion.4
  100.6 10.4 %all-to-all-start.1 = ((bf16[16,8,2048]{2,1,0:T(8,128)(2,1)}), bf16[16,8,2048]{2,1,0:T(8,128)(2,1)S(1)}, u32[]{:S(2)}, u32[]{:S(2)}) async-start(bf16[16,8,2048]{2,1,0:T(8,128)(2,1)} %fusion.4), calls=%async_computation.1 | async-start | bytes 1048576 | tf_op jit(solution)/shard_map/all_to_all | solution.py:432
  111.0 0.1 copy.38
  111.1 0.8 slice.32.mask
  112.0 0.7 fusion.38.extra
  112.7 0.6 add_convert_fusion.2.fresh_mask
  113.4 10.2 %shard_map.177 = bf16[64,1024]{1,0:T(8,128)(2,1)} custom-call(bf16[64,3072]{1,0:T(8,128)(2,1)} %shard_map.176.query.new_key.new_value, bf16[64,3072]{1,0:T(8,128)(2,1)} %shard_map.176.query.new_key.new_value, bf16[64,3072]{1,0:T(8,128)(2,1)} %shard_map.176.query.new_key.new_value, bf16[2048,2048]{1,0:T(8,128)(2,1)} %value.1, bf16[2048,2048]{1,0:T(8,128)(2,1)} %value.1, ...), custom_call_target="tpu_custom_call" | custom-call | tf_op jit(solution)/shard_map/pallas_call | solution.py:352
  123.6 1.8 all-to-all-done.1
  125.4 4.4 %convolution_convert_fusion.2.attn = bf16[64,2048]{1,0:T(8,128)(2,1)} fusion(bf16[64,1024]{1,0:T(8,128)(2,1)} %shard_map.177, bf16[2048,1024]{1,0:T(8,128)(2,1)} %all-gather.2.cloned.1.call-done), kind=kOutput, calls=%fused_computation.8 | convolution fusion | flops 268566528 | bytes 4587520 | tf_op jit(solution)/shard_map/tc,dc->td/dot_general | solution.py:414
  129.8 46.2 %shard_map.178 = (bf16[4,2,2,64,2176]{4,3,2,1,0:T(8,128)(2,1)}, f32[64,2048]{1,0:T(8,128)}) custom-call(bf16[64,2048]{1,0:T(8,128)(2,1)} %convolution_convert_fusion.2.attn, bf16[64,2048]{1,0:T(8,128)(2,1)} %tokens.1, f32[1,2048]{1,0:T(1,128)} %bitcast.55, bf16[64,128]{1,0:T(8,128)(2,1)} %fusion.38.extra), custom_call_target="tpu_custom_call" | custom-call | tf_op jit(solution)/shard_map/pallas_call | solution.py:298
  175.9 1.0 slice.34
  176.9 0.1 copy.41
  177.1 6.6 %fusion.2 = f32[1024,512]{1,0:T(8,128)} fusion(bf16[1024,2176]{1,0:T(8,128)(2,1)} %bitcast.53, bf16[1,2048,512]{2,1,0:T(8,128)(2,1)} %param.29), kind=kOutput, calls=%fused_computation.4 | convolution fusion | flops 2147483648 | bytes 8388608 | tf_op jit(solution)/shard_map/dot_general | solution.py:442
  183.6 0.1 fusion.29
  183.7 10.0 %multiply_convert_fusion = bf16[1024,2048]{1,0:T(8,128)(2,1)} fusion(f32[1024]{0:T(1024)S(1)} %fusion.29, bf16[1,512,2048]{2,1,0:T(8,128)(2,1)S(1)} %copy-done, f32[1024,512]{1,0:T(8,128)} %fusion.2, bf16[1,2048,512]{2,1,0:T(8,128)(2,1)} %param.30, bf16[1024,2176]{1,0:T(8,128)(2,1)} %bitcast.54), kind=kOutput, calls=%fused_computation | convolution fusion | flops 4306501632 | bytes 14684160 | tf_op jit(solution)/shard_map/dot_general | solution.py:445
  193.7 53.0 %shard_map.179 = f32[64,2048]{1,0:T(8,128)} custom-call(bf16[4,2,2,64,2048]{4,3,2,1,0:T(8,128)(2,1)} %bitcast.47), custom_call_target="tpu_custom_call" | custom-call | tf_op jit(solution)/shard_map/pallas_call | solution.py:207
  246.8 1.8 add_convert_fusion.1
  248.6 0.8 copy.44
  (38 shorter events, 0.5 us)
Async XLA Ops:
  7.2 176.5 %copy-start = (bf16[1,512,2048]{2,1,0:T(8,128)(2,1)S(1)}, bf16[1,512,2048]{2,1,0:T(8,128)(2,1)}, u32[]{:S(2)}) copy-start(bf16[1,512,2048]{2,1,0:T(8,128)(2,1)} %param.31) | copy-start | bytes 6291460
  7.2 11.2 %copy-start.8 = (s32[1,4]{1,0:T(1,128)S(1)}, s32[1,4]{1,0:T(1,128)}, u32[]{:S(2)}) copy-start(s32[1,4]{1,0:T(1,128)} %param.26) | copy-start | bytes 52
  7.2 11.5 %copy-start.9 = (s32[1,16]{1,0:T(1,128)S(1)}, s32[1,16]{1,0:T(1,128)}, u32[]{:S(2)}) copy-start(s32[1,16]{1,0:T(1,128)} %param.24) | copy-start | bytes 196
  7.2 11.5 %copy-start.10 = (s32[64,1]{0,1:T(1,128)S(1)}, s32[64,1]{0,1:T(1,128)}, u32[]{:S(2)}) copy-start(s32[64,1]{0,1:T(1,128)} %param.27) | copy-start | bytes 772
  7.2 11.8 %copy-start.7 = (s32[1,4]{1,0:T(1,128)S(1)}, s32[1,4]{1,0:T(1,128)}, u32[]{:S(2)}) copy-start(s32[1,4]{1,0:T(1,128)} %param.25) | copy-start | bytes 52
  7.2 23.4 %copy-start.2 = (bf16[128,1024]{1,0:T(8,128)(2,1)S(1)}, bf16[128,1024]{1,0:T(8,128)(2,1)}, u32[]{:S(2)}) copy-start(bf16[128,1024]{1,0:T(8,128)(2,1)} %param.21) | copy-start | bytes 786436
  7.2 23.4 %copy-start.3 = (bf16[128,1024]{1,0:T(8,128)(2,1)S(1)}, bf16[128,1024]{1,0:T(8,128)(2,1)}, u32[]{:S(2)}) copy-start(bf16[128,1024]{1,0:T(8,128)(2,1)} %param.20) | copy-start | bytes 786436
  7.2 23.4 %copy-start.4 = (bf16[128,1024]{1,0:T(8,128)(2,1)S(1)}, bf16[128,1024]{1,0:T(8,128)(2,1)}, u32[]{:S(2)}) copy-start(bf16[128,1024]{1,0:T(8,128)(2,1)} %param.19) | copy-start | bytes 786436
  7.3 118.1 %all-gather.2.cloned.1.call-start = ((), (), s32[]{:S(2)}) async-start(), calls=%async_computation.2 | async-start | bytes 4456448 | tf_op jit(solution)/shard_map/all_gather | solution.py:401
  11.1 19.5 %all-to-all-start = ((bf16[16,64,128]{2,1,0:T(8,128)(2,1)}), bf16[16,64,128]{2,1,0:T(8,128)(2,1)S(1)}, u32[]{:S(2)}, u32[]{:S(2)}) async-start(bf16[16,64,128]{2,1,0:T(8,128)(2,1)} %copy.36), calls=%async_computation | async-start | bytes 524288 | tf_op jit(solution)/shard_map/all_to_all | solution.py:404
  35.1 75.9 %copy-start.5 = (f32[64,8]{0,1:T(8,128)S(1)}, f32[64,8]{0,1:T(8,128)}, u32[]{:S(2)}) copy-start(f32[64,8]{0,1:T(8,128)} %param.33) | copy-start | bytes 6148
  35.1 75.9 %copy-start.6 = (s32[64,8]{0,1:T(8,128)S(1)}, s32[64,8]{0,1:T(8,128)}, u32[]{:S(2)}) copy-start(s32[64,8]{0,1:T(8,128)} %param.32) | copy-start | bytes 6148
  100.6 24.8 %all-to-all-start.1 = ((bf16[16,8,2048]{2,1,0:T(8,128)(2,1)}), bf16[16,8,2048]{2,1,0:T(8,128)(2,1)S(1)}, u32[]{:S(2)}, u32[]{:S(2)}) async-start(bf16[16,8,2048]{2,1,0:T(8,128)(2,1)} %fusion.4), calls=%async_computation.1 | async-start | bytes 1048576 | tf_op jit(solution)/shard_map/all_to_all | solution.py:432
  193.7 53.0 %copy-start.1 = (f32[64,2048]{1,0:T(8,128)S(1)}, f32[64,2048]{1,0:T(8,128)}, u32[]{:S(2)}) copy-start(f32[64,2048]{1,0:T(8,128)} %get-tuple-element.4) | copy-start | bytes 1572868
Sparse Core Ops, SparseCore 0:
  10.2 77.5 all-gather.1
